TPU v7x, 128 devices: a whole 4x4x4 slice. The times are simulated.
128 devices in a mesh: seq: 64 (over y, z_lo, x, core), tp: 2 (over z_hi).
Axes of the slice: x: 4, y: 4, z: 4 (z_hi: 2, z_lo: 2; z = z_hi * 2 + z_lo), core: 2. Of those that a mesh axis runs over, the one named last changes fastest.
Arguments:
- hidden_in: bfloat16 [16384, 2048], P('seq'), may hold values from -16 to 16
- attn_gain: float32 [2048], P('seq'), may hold values from 0.1 to 1.9
- w_query: float32 [2048, 2048], P('seq', 'tp'), may hold values from -0.25 to 0.25
- w_key: float32 [2048, 2048], P('seq', 'tp'), may hold values from -0.125 to 0.125
- w_value: float32 [2048, 2048], P('seq', 'tp'), may hold values from -0.125 to 0.125
- w_out: float32 [2048, 2048], P('tp', 'seq'), may hold values from -0.5 to 0.5
- ffn_gain: float32 [2048], P('seq'), may hold values from 0.1 to 1.9
- w_gate: float32 [2048, 5504], P('seq', 'tp'), may hold values from -0.125 to 0.125
- w_up: float32 [2048, 5504], P('seq', 'tp'), may hold values from -0.125 to 0.125
- w_down: float32 [5504, 2048], P('tp', 'seq'), may hold values from -0.15625 to 0.15625
- out_grad: bfloat16 [16384, 2048], P('seq'), may hold values from -16 to 16
Outputs:
- hidden_out: bfloat16 [16384, 2048], P('seq')
- in_grad: float32 [16384, 2048], P('seq')
- attn_gain_grad: float32 [2048], P('seq')
- w_query_grad: float32 [2048, 2048], P('seq', 'tp')
- w_key_grad: float32 [2048, 2048], P('seq', 'tp')
- w_value_grad: float32 [2048, 2048], P('seq', 'tp')
- w_out_grad: float32 [2048, 2048], P('tp', 'seq')
- ffn_gain_grad: float32 [2048], P('seq')
- w_gate_grad: float32 [2048, 5504], P('seq', 'tp')
- w_up_grad: float32 [2048, 5504], P('seq', 'tp')
- w_down_grad: float32 [5504, 2048], P('tp', 'seq')
All inputs are finite; a program needn't handle non-finite values.
Results may differ from a plain program's by a relative error of at most 0.017.
The roundings to bfloat16 on the way count: a program that leaves them out, or rounds other values in their place, can miss the bound.
Values may be sent and summed in bfloat16 or wider, within the bound.
A program may use at most 256 MiB of HBM per device.

v0:
```python
import math

import jax
import jax.numpy as jnp
from jax import lax
from jax.sharding import PartitionSpec as P

HD = 128
WINDOW = 1024


EPSILON = 1e-06
MASKED = -1e30


def shifted(value, axis, steps):
    count = lax.axis_size(axis)
    initial, last = (max(0, -steps), min(count, count - steps))
    return lax.ppermute(value, axis, [(source, source + steps) for source in range(initial, last)])


def rms_scale(values, gain):
    inverse = lax.rsqrt(jnp.mean(values * values, axis=-1, keepdims=True) + EPSILON)
    return values * inverse * gain


def pair_total(partial_value):
    return lax.psum(partial_value, "tp")


def split_heads(matrix, blocks_count, head_group):
    return jnp.moveaxis(matrix.reshape(matrix.shape[0], blocks_count, head_group, HD), 1, 0)


def join_heads(stacked):
    return jnp.moveaxis(stacked, 0, 1).reshape(stacked.shape[1], -1)


def per_device(
    hidden_in, attn_gain, w_query, w_key, w_value, w_out, ffn_gain, w_gate, w_up, w_down, out_grad
):
    half = jnp.bfloat16
    single = jnp.float32
    token_count = hidden_in.shape[0]
    seq_index = lax.axis_index("seq")
    reach_count = WINDOW // token_count
    query_full, key_full, value_full, out_full, gain_first = (
        lax.all_gather(w_query.astype(half), "seq", axis=0, tiled=True),
        lax.all_gather(w_key.astype(half), "seq", axis=0, tiled=True),
        lax.all_gather(w_value.astype(half), "seq", axis=0, tiled=True),
        lax.all_gather(w_out.astype(half), "seq", axis=1, tiled=True),
        lax.all_gather(attn_gain.astype(half), "seq", axis=0, tiled=True),
    )
    gate_full, up_full, down_full, gain_second = (
        lax.all_gather(w_gate.astype(half), "seq", axis=0, tiled=True),
        lax.all_gather(w_up.astype(half), "seq", axis=0, tiled=True),
        lax.all_gather(w_down.astype(half), "seq", axis=1, tiled=True),
        lax.all_gather(ffn_gain.astype(half), "seq", axis=0, tiled=True),
    )
    hidden_rows = hidden_in.astype(single)
    gain_one = gain_first.astype(single)
    first_in = rms_scale(hidden_rows, gain_one).astype(half)
    queries = jnp.dot(first_in, query_full, preferred_element_type=single).astype(half)
    keys_own = jnp.dot(first_in, key_full, preferred_element_type=single).astype(half)
    values_own = jnp.dot(first_in, value_full, preferred_element_type=single).astype(half)
    kv_own = jnp.stack([keys_own, values_own])
    earlier = [shifted(kv_own, "seq", offset) for offset in range(reach_count, 0, -1)]
    kv_all = jnp.concatenate(earlier + [kv_own], axis=1)
    key_count = kv_all.shape[1]
    query_pos = seq_index * token_count + jnp.arange(token_count, dtype=jnp.int32)
    key_pos = (
        seq_index * token_count - reach_count * token_count + jnp.arange(key_count, dtype=jnp.int32)
    )
    distance = query_pos[:, None] - key_pos[None, :]
    allowed = (key_pos[None, :] >= 0) & (distance >= 0) & (distance < WINDOW)
    local_heads = queries.shape[1] // HD
    head_group = math.gcd(local_heads, max(1, 2048 // token_count))
    blocks_count = local_heads // head_group
    score_scale = 1.0 / math.sqrt(HD)
    query_blocks = split_heads(queries, blocks_count, head_group)
    key_blocks = split_heads(kv_all[0], blocks_count, head_group)
    value_blocks = split_heads(kv_all[1], blocks_count, head_group)

    def scores_of(query_part, key_part):
        raw_scores = (
            jnp.einsum("qhd,khd->hqk", query_part, key_part, preferred_element_type=single)
            * score_scale
        )
        return jnp.where(allowed[None], raw_scores, MASKED)

    def attend(operands):
        query_part, key_part, value_part = operands
        scores = scores_of(query_part, key_part)
        row_max = jnp.max(scores, axis=-1, keepdims=True)
        expon = jnp.exp(scores - row_max)
        row_total = jnp.sum(expon, axis=-1, keepdims=True)
        probs = (expon / row_total).astype(half)
        mixed = jnp.einsum("hqk,khd->qhd", probs, value_part, preferred_element_type=single)
        return (mixed.astype(half), (row_max + jnp.log(row_total))[..., 0])

    attended_blocks, log_totals = lax.map(attend, (query_blocks, key_blocks, value_blocks))
    attended = join_heads(attended_blocks)
    mid_rows = hidden_rows + pair_total(jnp.dot(attended, out_full, preferred_element_type=single))
    gain_two = gain_second.astype(single)
    second_in = rms_scale(mid_rows, gain_two).astype(half)
    gate = jnp.dot(second_in, gate_full, preferred_element_type=single)
    up_proj = jnp.dot(second_in, up_full, preferred_element_type=single)
    hidden_ff = (jax.nn.silu(gate) * up_proj).astype(half)
    result_rows = mid_rows + pair_total(
        jnp.dot(hidden_ff, down_full, preferred_element_type=single)
    )
    hidden_out = result_rows.astype(half)
    gate_back, up_back, down_back, gain_two_back = (
        lax.all_gather(w_gate.astype(half), "seq", axis=0, tiled=True),
        lax.all_gather(w_up.astype(half), "seq", axis=0, tiled=True),
        lax.all_gather(w_down.astype(half), "seq", axis=1, tiled=True),
        lax.all_gather(ffn_gain.astype(half), "seq", axis=0, tiled=True),
    )
    query_back, key_back, value_back, out_back, gain_one_back = (
        lax.all_gather(w_query.astype(half), "seq", axis=0, tiled=True),
        lax.all_gather(w_key.astype(half), "seq", axis=0, tiled=True),
        lax.all_gather(w_value.astype(half), "seq", axis=0, tiled=True),
        lax.all_gather(w_out.astype(half), "seq", axis=1, tiled=True),
        lax.all_gather(attn_gain.astype(half), "seq", axis=0, tiled=True),
    )
    gain_two = gain_two_back.astype(single)
    gain_one = gain_one_back.astype(single)
    cot_rows = out_grad.astype(single)
    grad_ffn = cot_rows.astype(half)
    grad_hidden = jnp.einsum("td,fd->tf", grad_ffn, down_back, preferred_element_type=single)
    _, swiglu_back = jax.vjp(lambda gate_in, up_in: jax.nn.silu(gate_in) * up_in, gate, up_proj)
    grad_gate, grad_up = swiglu_back(grad_hidden)
    grad_gate = grad_gate.astype(half)
    grad_up = grad_up.astype(half)
    grad_second = pair_total(
        jnp.einsum("tf,df->td", grad_gate, gate_back, preferred_element_type=single)
        + jnp.einsum("tf,df->td", grad_up, up_back, preferred_element_type=single)
    )
    _, norm_two_back = jax.vjp(rms_scale, mid_rows, gain_two)
    grad_mid_part, ffn_gain_term = norm_two_back(grad_second)
    grad_mid = cot_rows + grad_mid_part
    grad_branch = grad_mid.astype(half)
    grad_attended = jnp.einsum(
        "td,cd->tc", grad_branch, out_back, preferred_element_type=single
    ).astype(half)
    grad_blocks = split_heads(grad_attended, blocks_count, head_group)

    def attend_back(operands):
        query_part, key_part, value_part, grad_part, log_part = operands
        scores = scores_of(query_part, key_part)
        probs = jnp.exp(scores - log_part[..., None])
        grad_values = jnp.einsum(
            "hqk,qhd->khd", probs.astype(half), grad_part, preferred_element_type=single
        )
        grad_probs = jnp.einsum(
            "qhd,khd->hqk", grad_part, value_part, preferred_element_type=single
        )
        inner = jnp.sum(probs * grad_probs, axis=-1, keepdims=True)
        grad_scores = (probs * (grad_probs - inner)).astype(half)
        grad_queries = (
            jnp.einsum("hqk,khd->qhd", grad_scores, key_part, preferred_element_type=single)
            * score_scale
        )
        grad_keys = (
            jnp.einsum("hqk,qhd->khd", grad_scores, query_part, preferred_element_type=single)
            * score_scale
        )
        return (grad_queries.astype(half), grad_keys, grad_values)

    grad_q_blocks, grad_k_blocks, grad_v_blocks = lax.map(
        attend_back, (query_blocks, key_blocks, value_blocks, grad_blocks, log_totals)
    )
    grad_queries = join_heads(grad_q_blocks)
    grad_kv = jnp.stack([join_heads(grad_k_blocks), join_heads(grad_v_blocks)])
    own_part = grad_kv[:, reach_count * token_count :]
    returned = own_part
    for offset in range(1, reach_count + 1):
        start_row = (reach_count - offset) * token_count
        returned = returned + shifted(
            grad_kv[:, start_row : start_row + token_count].astype(jnp.bfloat16), "seq", -offset
        ).astype(jnp.float32)
    grad_keys_own = returned[0].astype(half)
    grad_values_own = returned[1].astype(half)
    grad_first = pair_total(
        jnp.einsum("tc,dc->td", grad_queries, query_back, preferred_element_type=single)
        + jnp.einsum("tc,dc->td", grad_keys_own, key_back, preferred_element_type=single)
        + jnp.einsum("tc,dc->td", grad_values_own, value_back, preferred_element_type=single)
    )
    _, norm_one_back = jax.vjp(rms_scale, hidden_rows, gain_one)
    grad_rows_part, attn_gain_term = norm_one_back(grad_first)
    in_grad = grad_mid + grad_rows_part
    query_term = jnp.einsum("td,tc->dc", first_in, grad_queries, preferred_element_type=single)
    key_term = jnp.einsum("td,tc->dc", first_in, grad_keys_own, preferred_element_type=single)
    value_term = jnp.einsum("td,tc->dc", first_in, grad_values_own, preferred_element_type=single)
    out_term = jnp.einsum("tc,td->cd", attended, grad_branch, preferred_element_type=single)
    gate_term = jnp.einsum("td,tf->df", second_in, grad_gate, preferred_element_type=single)
    up_term = jnp.einsum("td,tf->df", second_in, grad_up, preferred_element_type=single)
    down_term = jnp.einsum("tf,td->fd", hidden_ff, grad_ffn, preferred_element_type=single)
    query_grad, key_grad, value_grad, out_proj_grad, attn_gain_grad = (
        lax.psum_scatter(query_term, "seq", scatter_dimension=0, tiled=True),
        lax.psum_scatter(key_term, "seq", scatter_dimension=0, tiled=True),
        lax.psum_scatter(value_term, "seq", scatter_dimension=0, tiled=True),
        lax.psum_scatter(out_term, "seq", scatter_dimension=1, tiled=True),
        lax.psum_scatter(attn_gain_term, "seq", scatter_dimension=0, tiled=True),
    )
    gate_grad, up_grad, down_grad, ffn_gain_grad = (
        lax.psum_scatter(gate_term, "seq", scatter_dimension=0, tiled=True),
        lax.psum_scatter(up_term, "seq", scatter_dimension=0, tiled=True),
        lax.psum_scatter(down_term, "seq", scatter_dimension=1, tiled=True),
        lax.psum_scatter(ffn_gain_term, "seq", scatter_dimension=0, tiled=True),
    )
    return (
        hidden_out,
        in_grad,
        attn_gain_grad,
        query_grad,
        key_grad,
        value_grad,
        out_proj_grad,
        ffn_gain_grad,
        gate_grad,
        up_grad,
        down_grad,
    )


def solution(mesh):
    placed = (
        P("seq", None),
        P("seq"),
        P("seq", "tp"),
        P("seq", "tp"),
        P("seq", "tp"),
        P("tp", "seq"),
        P("seq"),
        P("seq", "tp"),
        P("seq", "tp"),
        P("tp", "seq"),
        P("seq", None),
    )
    return jax.shard_map(
        per_device,
        mesh=mesh,
        in_specs=placed,
        out_specs=(
            P("seq", None),
            P("seq", None),
            P("seq"),
            P("seq", "tp"),
            P("seq", "tp"),
            P("seq", "tp"),
            P("tp", "seq"),
            P("seq"),
            P("seq", "tp"),
            P("seq", "tp"),
            P("tp", "seq"),
        ),
        check_vma=False,
    )
```

profile of v0, /device:TPU:1, one launch (start us, length us, event | category | flops | bytes accessed | tf_op | source)
XLA Modules:
  0.0 3458.9 jit_solution(12882840838084027553)
XLA Ops:
  17.5 142.3 %all-reduce.6 = (bf16[2048]{0:T(1024)(128)(2,1)S(1)}, bf16[2048]{0:T(1024)(128)(2,1)S(1)}) all-reduce(bf16[2048]{0:T(1024)(128)(2,1)S(1)} %dynamic-update-slice, bf16[2048]{0:T(1024)(128)(2,1)S(1)} %dynamic-update-slice.1), channel_id=1, replica_groups=mesh['seq'=64,'tp'=2] {'seq'}, use_global_device_ids=true, to_apply=%add | all-reduce | flops 4096 | bytes 16384
  165.3 61.8 %all-gather.8.cloned.1.call-done = bf16[2048,1024]{1,0:T(8,128)(2,1)} async-done(((bf16[32,1024]{1,0:T(8,128)(2,1)}), bf16[2048,1024]{1,0:T(8,128)(2,1)}) %all-gather.8.cloned.1.call-update) | async-done | bytes 4194320 | tf_op jit(solution)/shard_map/all_gather | solution.py:49
  245.8 164.6 %all-gather.12.cloned.1.call-done = bf16[2048,1024]{1,0:T(8,128)(2,1)} async-done(((bf16[32,1024]{1,0:T(8,128)(2,1)}), bf16[2048,1024]{1,0:T(8,128)(2,1)}) %all-gather.12.cloned.1.call-update) | async-done | bytes 4194320 | tf_op jit(solution)/shard_map/all_gather | solution.py:48
  442.2 75.2 %all-gather.14.cloned.1.call-done = bf16[1024,2048]{0,1:T(8,128)(2,1)} async-done(((bf16[1024,32]{0,1:T(8,128)(2,1)}), bf16[1024,2048]{0,1:T(8,128)(2,1)}) %all-gather.14.cloned.1.call-update) | async-done | bytes 4194320 | tf_op jit(solution)/shard_map/all_gather | solution.py:51
  525.1 67.2 %all-reduce.11.cloned.1.call-done = f32[256,2048]{1,0:T(8,128)} async-done(((f32[256,2048]{1,0:T(8,128)}), f32[256,2048]{1,0:T(8,128)}) %all-reduce.11.cloned.1.call-update) | async-done | bytes 2097168 | tf_op jit(solution)/shard_map/psum | solution.py:28
  595.5 115.3 %all-gather.18.cloned.1.call-done = bf16[2048,2752]{1,0:T(8,128)(2,1)} async-done(((bf16[32,2752]{1,0:T(8,128)(2,1)}), bf16[2048,2752]{1,0:T(8,128)(2,1)}) %all-gather.18.cloned.1.call-update) | async-done | bytes 11272208 | tf_op jit(solution)/shard_map/all_gather | solution.py:56
  721.5 107.7 %all-gather.16.cloned.1.call-done = bf16[2048,2752]{1,0:T(8,128)(2,1)} async-done(((bf16[32,2752]{1,0:T(8,128)(2,1)}), bf16[2048,2752]{1,0:T(8,128)(2,1)}) %all-gather.16.cloned.1.call-update) | async-done | bytes 11272208 | tf_op jit(solution)/shard_map/all_gather | solution.py:55
  829.2 10.8 fusion.54
  839.9 107.6 %all-gather.20.cloned.1.call-done = bf16[2752,2048]{0,1:T(8,128)(2,1)} async-done(((bf16[2752,32]{0,1:T(8,128)(2,1)}), bf16[2752,2048]{0,1:T(8,128)(2,1)}) %all-gather.20.cloned.1.call-update) | async-done | bytes 11272208 | tf_op jit(solution)/shard_map/all_gather | solution.py:57
  947.6 13.3 multiply_convert_fusion.1
  977.1 69.9 %all-reduce.13.cloned.1.call-done = f32[256,2048]{1,0:T(8,128)} async-done(((f32[256,2048]{1,0:T(8,128)}), f32[256,2048]{1,0:T(8,128)}) %all-reduce.13.cloned.1.call-update) | async-done | bytes 2097168 | tf_op jit(solution)/shard_map/psum | solution.py:28
  1121.0 11.0 collective-permute-done.6
  1172.6 12.5 fusion.61
  1185.2 13.2 fusion.60
  1198.8 12.8 fusion.59
  1212.2 87.6 %all-reduce.15.cloned.1.call-done = (f32[256,2048]{1,0:T(8,128)}, f32[256,2048]{1,0:T(8,128)}) async-done(((f32[256,2048]{1,0:T(8,128)}, f32[256,2048]{1,0:T(8,128)}), (f32[256,2048]{1,0:T(8,128)}, f32[256,2048]{1,0:T(8,128)})) %all-reduce.15.cloned.1.call-update) | async-done | bytes 4194320 | tf_op jit(solution)/shard_map/psum | solution.py:28
  1302.1 273.5 %all-reduce.4 = (f32[2048]{0:T(1024)S(1)}, f32[2048]{0:T(1024)S(1)}) all-reduce(f32[2048]{0:T(1024)S(1)} %get-tuple-element.54, f32[2048]{0:T(1024)S(1)} %get-tuple-element.52), channel_id=2, replica_groups=mesh['seq'=64,'tp'=2] {'seq'}, use_global_device_ids=true, to_apply=%region_12.13.clone | all-reduce | flops 4096 | bytes 32768
  1582.1 12.3 reduce-scatter.14.cloned.1.call-done
  1594.4 297.0 %reduce-scatter.8.cloned.1.call-done = f32[32,1024]{1,0:T(8,128)} async-done(((f32[2048,1024]{1,0:T(8,128)}), f32[32,1024]{1,0:T(8,128)}) %reduce-scatter.8.cloned.1.call-update) | async-done | bytes 131088 | tf_op jit(solution)/shard_map/reduce_scatter | solution.py:200
  1891.4 297.2 %reduce-scatter.12.cloned.1.call-done = f32[32,1024]{1,0:T(8,128)} async-done(((f32[2048,1024]{1,0:T(8,128)}), f32[32,1024]{1,0:T(8,128)}) %reduce-scatter.12.cloned.1.call-update) | async-done | bytes 131088 | tf_op jit(solution)/shard_map/reduce_scatter | solution.py:202
  2188.5 297.0 %reduce-scatter.10.cloned.1.call-done = f32[32,1024]{1,0:T(8,128)} async-done(((f32[2048,1024]{1,0:T(8,128)}), f32[32,1024]{1,0:T(8,128)}) %reduce-scatter.10.cloned.1.call-update) | async-done | bytes 131088 | tf_op jit(solution)/shard_map/reduce_scatter | solution.py:201
  2485.5 323.1 %reduce-scatter.20.cloned.1.call-done = f32[2752,32]{0,1:T(8,128)} async-done(((f32[2752,2048]{0,1:T(8,128)}), f32[2752,32]{0,1:T(8,128)}) %reduce-scatter.20.cloned.1.call-update) | async-done | bytes 352272 | tf_op jit(solution)/shard_map/reduce_scatter | solution.py:209
  2808.6 321.6 %reduce-scatter.18.cloned.1.call-done = f32[32,2752]{1,0:T(8,128)} async-done(((f32[2048,2752]{1,0:T(8,128)}), f32[32,2752]{1,0:T(8,128)}) %reduce-scatter.18.cloned.1.call-update) | async-done | bytes 352272 | tf_op jit(solution)/shard_map/reduce_scatter | solution.py:208
  3130.3 321.6 %reduce-scatter.16.cloned.1.call-done = f32[32,2752]{1,0:T(8,128)} async-done(((f32[2048,2752]{1,0:T(8,128)}), f32[32,2752]{1,0:T(8,128)}) %reduce-scatter.16.cloned.1.call-update) | async-done | bytes 352272 | tf_op jit(solution)/shard_map/reduce_scatter | solution.py:207
  (179 shorter events, 226.7 us)
Async XLA Ops:
  7.2 154.2 %all-gather.10.cloned.1.call-start = ((), (), s32[]{:S(2)}) async-start(), calls=%async_computation.8 | async-start | bytes 4259840 | tf_op jit(solution)/shard_map/all_gather | solution.py:50
  8.8 218.4 %all-gather.8.cloned.1.call-start = ((), (), s32[]{:S(2)}) async-start(), calls=%async_computation.7 | async-start | bytes 4259840 | tf_op jit(solution)/shard_map/all_gather | solution.py:49
  10.4 399.9 %all-gather.12.cloned.1.call-start = ((), (), s32[]{:S(2)}) async-start(), calls=%async_computation.9 | async-start | bytes 4259840 | tf_op jit(solution)/shard_map/all_gather | solution.py:48
  12.0 505.4 %all-gather.14.cloned.1.call-start = ((), (), s32[]{:S(2)}) async-start(), calls=%async_computation.10 | async-start | bytes 4259840 | tf_op jit(solution)/shard_map/all_gather | solution.py:51
  13.6 578.6 %all-reduce.11.cloned.1.call-start = ((), (), s32[]{:S(2)}) async-start(), calls=%async_computation.11 | async-start | bytes 4194304 | tf_op jit(solution)/shard_map/psum | solution.py:28
  231.7 184.2 %collective-permute-start = (bf16[2,256,1024]{2,1,0:T(8,128)(2,1)}, bf16[2,256,1024]{2,1,0:T(8,128)(2,1)}, u32[]{:S(2)}, u32[]{:S(2)}) collective-permute-start(bf16[2,256,1024]{2,1,0:T(8,128)(2,1)} %pad_maximum_fusion.1), channel_id=1, source_target_pairs={{0,8},{2,10},{4,12},{6,14},{8,16},{10,18},{12,20},{14,22},{16,24},... | collective-permute-start | bytes 3145736 | tf_op jit(solution)/shard_map/ppermute | solution.py:19
  236.3 181.1 %collective-permute-start.1 = (bf16[2,256,1024]{2,1,0:T(8,128)(2,1)}, bf16[2,256,1024]{2,1,0:T(8,128)(2,1)}, u32[]{:S(2)}, u32[]{:S(2)}) collective-permute-start(bf16[2,256,1024]{2,1,0:T(8,128)(2,1)} %pad_maximum_fusion.1), channel_id=1, source_target_pairs={{0,6},{2,8},{4,10},{6,12},{8,14},{10,16},{12,18},{14,20},{16,22},{... | collective-permute-start | bytes 3145736 | tf_op jit(solution)/shard_map/ppermute | solution.py:19
  240.3 179.7 %collective-permute-start.3 = (bf16[2,256,1024]{2,1,0:T(8,128)(2,1)}, bf16[2,256,1024]{2,1,0:T(8,128)(2,1)}, u32[]{:S(2)}, u32[]{:S(2)}) collective-permute-start(bf16[2,256,1024]{2,1,0:T(8,128)(2,1)} %pad_maximum_fusion.1), channel_id=1, source_target_pairs={{0,2},{2,4},{4,6},{6,8},{8,10},{10,12},{12,14},{14,16},{16,18},{18... | collective-permute-start | bytes 3145736 | tf_op jit(solution)/shard_map/ppermute | solution.py:19
  242.2 176.5 %collective-permute-start.2 = (bf16[2,256,1024]{2,1,0:T(8,128)(2,1)}, bf16[2,256,1024]{2,1,0:T(8,128)(2,1)}, u32[]{:S(2)}, u32[]{:S(2)}) collective-permute-start(bf16[2,256,1024]{2,1,0:T(8,128)(2,1)} %pad_maximum_fusion.1), channel_id=1, source_target_pairs={{0,4},{2,6},{4,8},{6,10},{8,12},{10,14},{12,16},{14,18},{16,20},{1... | collective-permute-start | bytes 3145736 | tf_op jit(solution)/shard_map/ppermute | solution.py:19
  522.4 188.4 %all-gather.18.cloned.1.call-start = ((), (), s32[]{:S(2)}) async-start(), calls=%async_computation.13 | async-start | bytes 11714560 | tf_op jit(solution)/shard_map/all_gather | solution.py:56
  523.1 306.0 %all-gather.16.cloned.1.call-start = ((), (), s32[]{:S(2)}) async-start(), calls=%async_computation.12 | async-start | bytes 11714560 | tf_op jit(solution)/shard_map/all_gather | solution.py:55
  524.0 423.5 %all-gather.20.cloned.1.call-start = ((), (), s32[]{:S(2)}) async-start(), calls=%async_computation.14 | async-start | bytes 11714560 | tf_op jit(solution)/shard_map/all_gather | solution.py:57
  524.8 522.2 %all-reduce.13.cloned.1.call-start = ((), (), s32[]{:S(2)}) async-start(), calls=%async_computation.15 | async-start | bytes 4194304 | tf_op jit(solution)/shard_map/psum | solution.py:28
  976.8 323.0 %all-reduce.15.cloned.1.call-start = ((), (), s32[]{:S(2)}) async-start(), calls=%async_computation.23 | async-start | bytes 8388608 | tf_op jit(solution)/shard_map/psum | solution.py:28
  1092.3 28.8 collective-permute-start.7
  1093.6 38.5 %collective-permute-start.6 = (bf16[2,256,1024]{1,2,0:T(8,128)(2,1)}, bf16[2,256,1024]{1,2,0:T(8,128)(2,1)}, u32[]{:S(2)}, u32[]{:S(2)}) collective-permute-start(bf16[2,256,1024]{1,2,0:T(8,128)(2,1)} %get-tuple-element.79), channel_id=1, source_target_pairs={{6,0},{8,2},{10,4},{12,6},{14,8},{16,10},{18,12},{20,14},{22,16},{... | collective-permute-start | bytes 3145736 | tf_op jit(solution)/shard_map/ppermute | solution.py:19
  1094.9 45.0 %collective-permute-start.5 = (bf16[2,256,1024]{1,2,0:T(8,128)(2,1)}, bf16[2,256,1024]{1,2,0:T(8,128)(2,1)}, u32[]{:S(2)}, u32[]{:S(2)}) collective-permute-start(bf16[2,256,1024]{1,2,0:T(8,128)(2,1)} %get-tuple-element.80), channel_id=1, source_target_pairs={{4,0},{6,2},{8,4},{10,6},{12,8},{14,10},{16,12},{18,14},{20,16},{2... | collective-permute-start | bytes 3145736 | tf_op jit(solution)/shard_map/ppermute | solution.py:19
  1148.2 446.2 %reduce-scatter.14.cloned.1.call-start = ((), (), s32[]{:S(2)}) async-start(), calls=%async_computation.19 | async-start | bytes 8519680 | tf_op jit(solution)/shard_map/reduce_scatter | solution.py:203
  1154.7 736.7 %reduce-scatter.8.cloned.1.call-start = ((), (), s32[]{:S(2)}) async-start(), calls=%async_computation.16 | async-start | bytes 8519680 | tf_op jit(solution)/shard_map/reduce_scatter | solution.py:200
  1160.6 1027.9 %reduce-scatter.12.cloned.1.call-start = ((), (), s32[]{:S(2)}) async-start(), calls=%async_computation.18 | async-start | bytes 8519680 | tf_op jit(solution)/shard_map/reduce_scatter | solution.py:202
  1166.7 1318.8 %reduce-scatter.10.cloned.1.call-start = ((), (), s32[]{:S(2)}) async-start(), calls=%async_computation.17 | async-start | bytes 8519680 | tf_op jit(solution)/shard_map/reduce_scatter | solution.py:201
  1172.6 1636.0 %reduce-scatter.20.cloned.1.call-start = ((), (), s32[]{:S(2)}) async-start(), calls=%async_computation.22 | async-start | bytes 23429120 | tf_op jit(solution)/shard_map/reduce_scatter | solution.py:209
  1185.2 1945.1 %reduce-scatter.18.cloned.1.call-start = ((), (), s32[]{:S(2)}) async-start(), calls=%async_computation.21 | async-start | bytes 23429120 | tf_op jit(solution)/shard_map/reduce_scatter | solution.py:208
  1198.4 2253.5 %reduce-scatter.16.cloned.1.call-start = ((), (), s32[]{:S(2)}) async-start(), calls=%async_computation.20 | async-start | bytes 23429120 | tf_op jit(solution)/shard_map/reduce_scatter | solution.py:207
  (29 other events, 709.3 us)
Sparse Core Ops, SparseCore 0:
  10.3 109.5 all-gather.9
  122.1 104.9 all-gather.7
  229.4 180.8 all-gather.11
  412.5 104.9 all-gather.13
  522.5 69.7 all-reduce.10
  594.5 116.1 all-gather.17
  713.2 115.9 all-gather.15
  831.6 115.9 all-gather.19
  977.0 69.9 all-reduce.12
  1148.3 151.4 all-reduce.14
  1302.9 291.4 reduce-scatter.13
  1597.3 293.9 reduce-scatter.7
  1894.4 294.0 reduce-scatter.11
  2191.5 294.0 reduce-scatter.9
  2488.5 320.0 reduce-scatter.19
  2811.6 318.6 reduce-scatter.17
  3133.3 318.5 reduce-scatter.15
where the time goes:
time: 3470 us; the launch traced here: 3460 us
  waiting for transfers between devices  2760 us (80%)
  blocking collectives  416 us (12%)
  matrix products  173 us (5%)
  other arithmetic  42.4 us (1%)
    unnamed x2, blocking collectives  416 us
    reduce_scatter x1, waiting for transfers between devices, per_device(): lax.psum_scatter(down_term, 'seq', scatter_dimension=1, tiled=True)  323 us
    reduce_scatter x1, waiting for transfers between devices, per_device(): lax.psum_scatter(up_term, 'seq', scatter_dimension=0, tiled=True)  322 us
    reduce_scatter x1, waiting for transfers between devices, per_device(): lax.psum_scatter(gate_term, 'seq', scatter_dimension=0, tiled=True)  322 us
    reduce_scatter x1, waiting for transfers between devices, per_device(): lax.psum_scatter(value_term, 'seq', scatter_dimension=0, tiled=True)  297 us
    reduce_scatter x1, waiting for transfers between devices, per_device(): lax.psum_scatter(key_term, 'seq', scatter_dimension=0, tiled=True)  297 us
    reduce_scatter x1, waiting for transfers between devices, per_device(): lax.psum_scatter(query_term, 'seq', scatter_dimension=0, tiled=True)  297 us
    psum x3, waiting for transfers between devices, pair_total(): return lax.psum(partial_value, 'tp')  225 us
  transfers between devices with their start and end apart: 25, of which 20 were waited for; matrix products, arithmetic and copies ran while one was open for 5% of the time, Pallas kernels for 0%

commit v1 on v0

v1 whole, which is shorter than its diff:
```python
import functools
import math

import jax
import jax.numpy as jnp
from jax import lax
from jax.experimental import pallas as pl
from jax.experimental.pallas import tpu as pltpu
from jax.sharding import PartitionSpec as P

HD = 128
WINDOW = 1024
EPSILON = 1e-06
MASKED = -1e30
MESH = pl.DeviceIdType.MESH
HALF = jnp.bfloat16
SINGLE = jnp.float32
VMEM_LIMIT = 60 * 2**20


def coords():
    s = lax.axis_index("seq")
    t = lax.axis_index("tp")
    return lax.rem(lax.div(s, 2), 4), lax.div(s, 16), lax.rem(lax.div(s, 8), 2), lax.rem(s, 2), t


def device(x, y, z, c, t):
    return (((y * 2 + z) * 4 + x) * 2 + c, t)


def up(v):
    return lax.rem(v + 1, 4)


def down(v):
    return lax.rem(v + 3, 4)


def across(v):
    return lax.rem(v + 2, 4)


def chip_shift(steps):
    s = lax.axis_index("seq")
    return (lax.rem(s + 2 * steps + 64, 64), lax.axis_index("tp"))


def greet(partners):
    barrier = pltpu.get_barrier_semaphore()
    for partner in partners:
        pl.semaphore_signal(barrier, inc=1, device_id=partner, device_id_type=MESH)
    pl.semaphore_wait(barrier, len(partners))


class Sems:
    def __init__(self, send, recv):
        self.send, self.recv, self.used, self.started = send, recv, 0, []

    def copy(self, src, dst, dev):
        i = self.used
        self.used += 1
        return pltpu.make_async_remote_copy(
            src, dst, self.send.at[i], self.recv.at[i], device_id=dev, device_id_type=MESH
        )

    def start(self, *copies):
        for copy in copies:
            copy.start()
            self.started.append(copy)

    def finish(self):
        for copy in self.started:
            copy.wait_send()


def gather_steps(w_in, out, sems, local_sem):
    x, y, z, c, t = coords()
    mine = pltpu.make_async_copy(w_in.at[c], out.at[y, z, x, c], local_sem)
    swap = sems.copy(w_in.at[1 - c], out.at[y, z, x, c], device(x, y, z, 1 - c, t))
    pieces = []
    for h in range(2):
        if h == 0:
            at = lambda a, zs, b, h=h: out.at[a, zs, b, h]
            a, b = y, x
            to_a = lambda v: device(x, v, z, c, t)
            to_b = lambda v: device(v, y, z, c, t)
        else:
            at = lambda a, zs, b, h=h: out.at[b, zs, a, h]
            a, b = x, y
            to_a = lambda v: device(v, y, z, c, t)
            to_b = lambda v: device(x, v, z, c, t)
        full = slice(None)

        def copy(src, dev):
            return sems.copy(src, src, dev)

        pieces.append(
            dict(
                z=copy(out.at[y, z, x, h], device(x, y, 1 - z, c, t)),
                a1p=copy(at(a, full, b), to_a(up(a))),
                a1m=copy(at(a, full, b), to_a(down(a))),
                a2p=copy(at(down(a), 0, b), to_a(up(a))),
                a2m=copy(at(up(a), 1, b), to_a(down(a))),
                b1p=copy(at(full, full, b), to_b(up(b))),
                b1m=copy(at(full, full, b), to_b(down(b))),
                b2p=copy(at(slice(0, 2), full, down(b)), to_b(up(b))),
                b2m=copy(at(slice(2, 4), full, up(b)), to_b(down(b))),
            )
        )

    def step0():
        mine.start()
        sems.start(swap)

    def step1():
        mine.wait()
        swap.wait_recv()
        for p in pieces:
            sems.start(p["z"])

    def step2():
        for p in pieces:
            p["z"].wait_recv()
            sems.start(p["a1p"], p["a1m"])

    def step3():
        for p in pieces:
            p["a1p"].wait_recv()
            sems.start(p["a2p"])
            p["a1m"].wait_recv()
            sems.start(p["a2m"])

    def step4():
        for p in pieces:
            p["a2p"].wait_recv()
            p["a2m"].wait_recv()
            sems.start(p["b1p"], p["b1m"])

    def step5():
        for p in pieces:
            p["b1p"].wait_recv()
            sems.start(p["b2p"])
            p["b1m"].wait_recv()
            sems.start(p["b2m"])

    def step6():
        for p in pieces:
            p["b2p"].wait_recv()
            p["b2m"].wait_recv()

    return [step0, step1, step2, step3, step4, step5, step6]


def halo_steps(hid, cot, xh, cots, sems, local_sems):
    x, y, z, c, t = coords()
    core = device(x, y, z, 1 - c, t)
    pair = device(x, y, z, c, 1 - t)
    locals_ = [
        pltpu.make_async_copy(hid, cots.at[0, c], local_sems.at[0]),
        pltpu.make_async_copy(cot, cots.at[1, c], local_sems.at[1]),
    ]
    swaps = [
        sems.copy(hid, cots.at[0, c], core),
        sems.copy(cot, cots.at[1, c], core),
    ]
    parts = []
    for j, shift in ((1, 1), (0, 2)):
        slot, other = xh.at[j, c, t], xh.at[j, c, 1 - t]
        parts.append(
            dict(
                first=sems.copy(hid.at[t], slot, chip_shift(shift)),
                pair=sems.copy(slot, slot, pair),
                core=sems.copy(slot, slot, core),
                both=sems.copy(other, other, core),
            )
        )

    def step0():
        for copy in locals_:
            copy.start()
        sems.start(*[p["first"] for p in parts])
        sems.start(*swaps)

    def step1():
        for p in parts:
            p["first"].wait_recv()
            sems.start(p["pair"], p["core"])

    def step2():
        for p in parts:
            p["pair"].wait_recv()
            sems.start(p["both"])

    def step3():
        for p in parts:
            p["core"].wait_recv()
            p["both"].wait_recv()
        for copy in locals_:
            copy.wait()
        for copy in swaps:
            copy.wait_recv()

    return [step0, step1, step2, step3]


def neighbours():
    x, y, z, c, t = coords()
    return [
        device(up(x), y, z, c, t),
        device(down(x), y, z, c, t),
        device(x, up(y), z, c, t),
        device(x, down(y), z, c, t),
        device(x, y, 1 - z, c, t),
        device(x, y, z, 1 - c, t),
    ]


def gather_kernel(chunks, *refs):
    w_in, (hid, cot) = refs[:chunks], refs[chunks : chunks + 2]
    rest = refs[chunks + 2 :]
    w_out, (xh, cots) = rest[:chunks], rest[chunks : chunks + 2]
    send, recv, local_sems = rest[chunks + 2 :]
    x, y, z, c, t = coords()
    sems = Sems(send, recv)
    greet(
        neighbours()
        + [device(x, y, z, c, 1 - t), chip_shift(1), chip_shift(-1), chip_shift(2), chip_shift(-2)]
    )
    halo = halo_steps(hid, cot, xh, cots, sems, local_sems)
    chunk_steps = [
        gather_steps(w_in[i], w_out[i], sems, local_sems.at[2 + i]) for i in range(chunks)
    ]
    halo[0]()
    for steps in chunk_steps:
        steps[0]()
    for steps in chunk_steps:
        steps[1]()
    order = []
    for i in range(chunks):
        for j in range(2, 7):
            order.append((2 * i + j, i, j))
    done_halo = 1
    for tick in sorted({o[0] for o in order}):
        for when, i, j in sorted(order):
            if when == tick:
                chunk_steps[i][j]()
        if tick >= 4 and done_halo < 4:
            halo[done_halo]()
            done_halo += 1
    while done_halo < 4:
        halo[done_halo]()
        done_halo += 1
    sems.finish()


def gather_all(chunks, hid, cot):
    n = len(chunks)
    features = hid.shape[-1]
    anywhere = pl.BlockSpec(memory_space=pl.ANY)
    copies = 19 * n + 10
    return pl.pallas_call(
        functools.partial(gather_kernel, n),
        out_shape=[jax.ShapeDtypeStruct((4, 2, 4, 2, 32, w.shape[-1]), HALF) for w in chunks]
        + [
            jax.ShapeDtypeStruct((2, 2, 2, 128, features), HALF),
            jax.ShapeDtypeStruct((2, 2, 2, 128, features), HALF),
        ],
        in_specs=[anywhere] * (n + 2),
        out_specs=[anywhere] * (n + 2),
        scratch_shapes=[
            pltpu.SemaphoreType.DMA((copies,)),
            pltpu.SemaphoreType.DMA((copies,)),
            pltpu.SemaphoreType.DMA((2 + n,)),
        ],
        compiler_params=pltpu.CompilerParams(
            collective_id=0, has_side_effects=True, vmem_limit_bytes=VMEM_LIMIT
        ),
    )(*chunks, hid.reshape(2, 128, features), cot.reshape(2, 128, features))


def add_blocks(target, index, sources):
    total = target(index[0]).astype(SINGLE)
    for source in sources:
        total = total + source
    return total


def scatter_steps(g, out, bufs, sems, local_sems, final_swap):
    x, y, z, c, t = coords()
    full = slice(None)
    pieces = []
    for h in range(2):
        r2, r1, q2, q1, rz, tt, ss = bufs[7 * h : 7 * h + 7]
        if h == 0:
            a, b = y, x
            to_a = lambda v: device(x, v, z, c, t)
            to_b = lambda v: device(v, y, z, c, t)
            at = lambda ref, aa, zz: ref.at[aa, zz]
            at_g = lambda aa, bb, h=h: g.at[aa, :, bb, h]
        else:
            a, b = x, y
            to_a = lambda v: device(v, y, z, c, t)
            to_b = lambda v: device(x, v, z, c, t)
            at = lambda ref, aa, zz: ref.at[zz, aa]
            at_g = lambda aa, bb, h=h: g.at[bb, :, aa, h]
        low, high = slice(0, 2), slice(2, 4)
        p = dict(
            load_p=pltpu.make_async_copy(at_g(low, up(b)), tt.at[0], local_sems.at[3 * h]),
            load_m=pltpu.make_async_copy(at_g(high, down(b)), tt.at[1], local_sems.at[3 * h + 1]),
            load_s=pltpu.make_async_copy(at_g(full, b), ss, local_sems.at[3 * h + 2]),
            x2p=sems.copy(at_g(low, across(b)), r2.at[0], to_b(up(b))),
            x2m=sems.copy(at_g(high, across(b)), r2.at[1], to_b(down(b))),
            x1ap=sems.copy(at_g(high, up(b)), at(r1.at[0], high, full), to_b(up(b))),
            x1am=sems.copy(at_g(low, down(b)), at(r1.at[1], low, full), to_b(down(b))),
            x1bp=sems.copy(tt.at[0], at(r1.at[0], low, full), to_b(up(b))),
            x1bm=sems.copy(tt.at[1], at(r1.at[1], high, full), to_b(down(b))),
            y2p=sems.copy(at(ss, across(a), 0), q2.at[0], to_a(up(a))),
            y2m=sems.copy(at(ss, across(a), 1), q2.at[1], to_a(down(a))),
            y1ap=sems.copy(at(ss, up(a), 1), q1.at[0, 1], to_a(up(a))),
            y1am=sems.copy(at(ss, down(a), 0), q1.at[1, 0], to_a(down(a))),
            y1bp=sems.copy(at(ss, up(a), 0), q1.at[0, 0], to_a(up(a))),
            y1bm=sems.copy(at(ss, down(a), 1), q1.at[1, 1], to_a(down(a))),
            z=sems.copy(at(ss, a, 1 - z), rz, device(x, y, 1 - z, c, t)),
        )
        p.update(r2=r2, r1=r1, q2=q2, q1=q1, rz=rz, tt=tt, ss=ss, a=a, at=at, h=h)
        pieces.append(p)

    def plus(ref, *others):
        total = ref[...].astype(SINGLE)
        for other in others:
            total = total + other[...].astype(SINGLE)
        ref[...] = total.astype(HALF)

    def step0():
        for p in pieces:
            sems.start(p["x2p"], p["x2m"])
            p["load_p"].start()
            p["load_m"].start()
            p["load_s"].start()
        for p in pieces:
            sems.start(p["x1ap"], p["x1am"])

    def step1():
        for p in pieces:
            for d, load, came, go in ((0, "load_p", "x2p", "x1bp"), (1, "load_m", "x2m", "x1bm")):
                p[load].wait()
                p[came].wait_recv()

                def body(i, carry, p=p, d=d):
                    u, v = lax.div(i, 2), lax.rem(i, 2)
                    plus(p["tt"].at[d, u, v], p["r2"].at[d, u, v])
                    return carry

                lax.fori_loop(0, 4, body, 0)
                sems.start(p[go])

    def step2():
        for p in pieces:
            p["load_s"].wait()
            for name in ("x1ap", "x1am", "x1bp", "x1bm"):
                p[name].wait_recv()
            inner = p["ss"].shape[1]

            def body(i, carry, p=p, inner=inner):
                u, v = lax.div(i, inner), lax.rem(i, inner)
                plus(p["ss"].at[u, v], p["r1"].at[0, u, v], p["r1"].at[1, u, v])
                return carry

            lax.fori_loop(0, 8, body, 0)
            sems.start(p["y2p"], p["y2m"], p["y1ap"], p["y1am"])

    def step3():
        for p in pieces:
            p["y2p"].wait_recv()
            plus(p["at"](p["ss"], up(p["a"]), 0), p["q2"].at[0])
            sems.start(p["y1bp"])
            p["y2m"].wait_recv()
            plus(p["at"](p["ss"], down(p["a"]), 1), p["q2"].at[1])
            sems.start(p["y1bm"])

    def step4():
        for p in pieces:
            for name in ("y1ap", "y1am", "y1bp", "y1bm"):
                p[name].wait_recv()
            for zz in range(2):
                plus(p["at"](p["ss"], p["a"], zz), p["q1"].at[0, zz], p["q1"].at[1, zz])
            sems.start(p["z"])

    def step5():
        for p in pieces:
            p["z"].wait_recv()
            total = p["at"](p["ss"], p["a"], z)[...].astype(SINGLE) + p["rz"][...].astype(SINGLE)
            final_swap[p["h"]] = total
        out[c] = final_swap[c]
        copy = sems.copy(final_swap.at[1 - c], out.at[c], device(x, y, z, 1 - c, t))
        sems.start(copy)

        def step6():
            copy.wait_recv()

        steps.append(step6)

    steps = [step0, step1, step2, step3, step4, step5]
    return steps


def scatter_kernel(chunks, *refs):
    g = refs[:chunks]
    out = refs[chunks : 2 * chunks]
    bufs = refs[2 * chunks : 2 * chunks + 14 * chunks]
    finals = refs[16 * chunks : 17 * chunks]
    send, recv, local_sems = refs[17 * chunks :]
    sems = Sems(send, recv)
    greet(neighbours())
    all_steps = [
        scatter_steps(
            g[i], out[i], bufs[14 * i : 14 * i + 14], sems, local_sems.at[i], finals[i]
        )
        for i in range(chunks)
    ]
    for tick in range(chunks + 8):
        for i in range(chunks):
            j = tick - i
            if 0 <= j < len(all_steps[i]):
                all_steps[i][j]()
    sems.finish()


def scatter_all(chunks):
    n = len(chunks)
    bufs = []
    for g in chunks:
        w = g.shape[-1]
        for h in range(2):
            wide = (4, 2) if h == 0 else (2, 4)
            bufs += [
                pltpu.VMEM((2, 2, 2, 32, w), HALF),
                pltpu.VMEM((2, *wide, 32, w), HALF),
                pltpu.VMEM((2, 32, w), HALF),
                pltpu.VMEM((2, 2, 32, w), HALF),
                pltpu.VMEM((32, w), HALF),
                pltpu.VMEM((2, 2, 2, 32, w), HALF),
                pltpu.VMEM((*wide, 32, w), HALF),
            ]
    anywhere = pl.BlockSpec(memory_space=pl.ANY)
    in_vmem = pl.BlockSpec(memory_space=pltpu.VMEM)
    copies = 27 * n
    return pl.pallas_call(
        functools.partial(scatter_kernel, n),
        out_shape=[jax.ShapeDtypeStruct((2, 32, g.shape[-1]), SINGLE) for g in chunks],
        in_specs=[anywhere] * n,
        out_specs=[in_vmem] * n,
        scratch_shapes=bufs
        + [pltpu.VMEM((2, 32, g.shape[-1]), SINGLE) for g in chunks]
        + [
            pltpu.SemaphoreType.DMA((copies,)),
            pltpu.SemaphoreType.DMA((copies,)),
            pltpu.SemaphoreType.DMA((n, 6)),
        ],
        compiler_params=pltpu.CompilerParams(
            collective_id=6, has_side_effects=True, vmem_limit_bytes=VMEM_LIMIT
        ),
    )(*[g.reshape(4, 2, 4, 2, 32, g.shape[-1]) for g in chunks])


PARTS = 4
ROWS = 16


def sum_kernel(post, n_in, n_out, spread, *refs):
    part, ins = refs[0], refs[1 : 1 + n_in]
    outs = refs[1 + n_in : 1 + n_in + n_out]
    rest = refs[1 + n_in + n_out :]
    shared = None
    if spread:
        shared, rest = rest[0], rest[1:]
    to_core, from_core, to_pair, from_pair, send, recv = rest
    x, y, z, c, t = coords()
    sems = Sems(send, recv)
    core, pair = device(x, y, z, 1 - c, t), device(x, y, z, c, 1 - t)
    size = to_core.shape[0] // PARTS
    greet([core, pair])
    rows = [pl.ds(i * size, size) for i in range(PARTS)]
    core_copies = [sems.copy(to_core.at[r], from_core.at[r], core) for r in rows]
    pair_copies = [sems.copy(to_pair.at[r], from_pair.at[r], pair) for r in rows]

    def over(i, fn):
        def body(k, carry):
            fn(pl.ds(pl.multiple_of(i * size + k * ROWS, ROWS), ROWS))
            return carry

        lax.fori_loop(0, size // ROWS, body, 0)

    def first(r):
        to_core[r, :] = part[1 - c, r, :].astype(HALF)

    def second(r):
        to_pair[r, :] = (part[c, r, :] + from_core[r, :].astype(SINGLE)).astype(HALF)

    def third(r):
        total = to_pair[r, :].astype(SINGLE) + from_pair[r, :].astype(SINGLE)
        sent = post(r, total, ins, outs)
        if spread:
            shared[c, r, :] = sent.astype(HALF)

    for i in range(PARTS):
        over(i, first)
        sems.start(core_copies[i])
    for i in range(PARTS):
        core_copies[i].wait_recv()
        over(i, second)
        sems.start(pair_copies[i])
    spreads = []
    for i in range(PARTS):
        pair_copies[i].wait_recv()
        over(i, third)
        if spread:
            copy = sems.copy(shared.at[c, rows[i]], shared.at[c, rows[i]], core)
            sems.start(copy)
            spreads.append(copy)
    for copy in spreads:
        copy.wait_recv()
    sems.finish()


def sum_call(post, collective_id, part, ins, outs, spread):
    tokens, features = part.shape[0] // 2, part.shape[1]
    in_vmem = pl.BlockSpec(memory_space=pltpu.VMEM)
    out_shape = list(outs)
    if spread:
        out_shape.append(jax.ShapeDtypeStruct((2, tokens, features), HALF))
    copies = 3 * PARTS
    return pl.pallas_call(
        functools.partial(sum_kernel, post, len(ins), len(outs), spread),
        out_shape=out_shape,
        in_specs=[in_vmem] * (1 + len(ins)),
        out_specs=[in_vmem] * len(out_shape),
        scratch_shapes=[pltpu.VMEM((tokens, features), HALF) for _ in range(4)]
        + [pltpu.SemaphoreType.DMA((copies,)), pltpu.SemaphoreType.DMA((copies,))],
        compiler_params=pltpu.CompilerParams(
            collective_id=collective_id, has_side_effects=True, vmem_limit_bytes=VMEM_LIMIT
        ),
    )(part.reshape(2, tokens, features), *ins)


def post_mid(r, total, ins, outs):
    hidden, gain = ins
    (mid_out,) = outs
    mid = hidden[r, :].astype(SINGLE) + total
    mid_out[r, :] = mid
    inverse = lax.rsqrt(jnp.mean(mid * mid, axis=-1, keepdims=True) + EPSILON)
    return mid * inverse * gain[...]


def post_out(r, total, ins, outs):
    outs[0][r, :] = (ins[0][r, :] + total).astype(HALF)


def norm_back(grad, values, gain):
    inverse = lax.rsqrt(jnp.mean(values * values, axis=-1, keepdims=True) + EPSILON)
    scaled = grad * gain
    slope = jnp.mean(scaled * values, axis=-1, keepdims=True)
    gain_term = jnp.sum(grad * values * inverse, axis=0, keepdims=True)
    return inverse * scaled - values * (inverse * inverse * inverse * slope), gain_term


def add_gain_term(gain_out, r, term):
    gain_out[...] += term


def post_mid_back(r, total, ins, outs):
    mid, cot, gain = ins
    gmid_out, gain_out = outs
    part, term = norm_back(total, mid[r, :], gain[...])
    gmid = cot[r, :].astype(SINGLE) + part
    gmid_out[r, :] = gmid
    gain_out[r, :] = jnp.broadcast_to(term, (ROWS, term.shape[1]))
    return gmid


def post_in_back(r, total, ins, outs):
    hidden, gmid, gain = ins
    grad_out, gain_out = outs
    part, term = norm_back(total, hidden[r, :].astype(SINGLE), gain[...])
    grad_out[r, :] = gmid[r, :] + part
    gain_out[r, :] = jnp.broadcast_to(term, (ROWS, term.shape[1]))


def return_kernel(own, far, out, got, send, recv):
    sems = Sems(send, recv)
    greet([chip_shift(1), chip_shift(-1), chip_shift(2), chip_shift(-2)])
    copies = [
        sems.copy(far.at[1], got.at[1], chip_shift(-1)),
        sems.copy(far.at[0], got.at[0], chip_shift(-2)),
    ]
    sems.start(*copies)
    for copy in copies:
        copy.wait_recv()

    def body(i, carry):
        r = pl.ds(pl.multiple_of(i * 32, 32), 32)
        total = own[r, :] + got[1, r, :].astype(SINGLE) + got[0, r, :].astype(SINGLE)
        out[r, :] = total.astype(HALF)
        return carry

    lax.fori_loop(0, own.shape[0] // 32, body, 0)
    sems.finish()


def return_call(own, far):
    in_vmem = pl.BlockSpec(memory_space=pltpu.VMEM)
    return pl.pallas_call(
        return_kernel,
        out_shape=jax.ShapeDtypeStruct(own.shape, HALF),
        in_specs=[in_vmem] * 2,
        out_specs=in_vmem,
        scratch_shapes=[
            pltpu.VMEM(far.shape, HALF),
            pltpu.SemaphoreType.DMA((2,)),
            pltpu.SemaphoreType.DMA((2,)),
        ],
        compiler_params=pltpu.CompilerParams(
            collective_id=5, has_side_effects=True, vmem_limit_bytes=VMEM_LIMIT
        ),
    )(own, far)


QB = 256
KB = QB + WINDOW
SCALE = 1.0 / math.sqrt(HD)


def allowed_pairs(base):
    row = lax.broadcasted_iota(jnp.int32, (QB, KB), 0)
    col = lax.broadcasted_iota(jnp.int32, (QB, KB), 1)
    return (col > row) & (col <= row + WINDOW) & (col + base >= 0)


def product(a, b, dims):
    return lax.dot_general(a, b, (dims, ((), ())), preferred_element_type=SINGLE)


def attend_kernel(chip_ref, q_ref, k_ref, v_ref, o_ref, lse_ref):
    i = pl.program_id(1)
    keys = pl.ds(pl.multiple_of(i * QB, QB), KB)
    base = (chip_ref[0] - 2) * 512 + i * QB
    scores = product(q_ref[...], k_ref[keys, :], ((1,), (1,))) * SCALE
    scores = jnp.where(allowed_pairs(base), scores, MASKED)
    row_max = jnp.max(scores, axis=-1, keepdims=True)
    expon = jnp.exp(scores - row_max)
    row_total = jnp.sum(expon, axis=-1, keepdims=True)
    probs = (expon * (1.0 / row_total)).astype(HALF)
    o_ref[...] = product(probs, v_ref[keys, :], ((1,), (0,))).astype(HALF)
    lse_ref[...] = jnp.broadcast_to(row_max + jnp.log(row_total), lse_ref.shape)


def attend(chip, q, k, v):
    tokens, width = q.shape
    heads = width // HD
    return pl.pallas_call(
        attend_kernel,
        out_shape=[
            jax.ShapeDtypeStruct((tokens, width), HALF),
            jax.ShapeDtypeStruct((tokens, width), SINGLE),
        ],
        grid=(heads, tokens // QB),
        in_specs=[
            pl.BlockSpec(memory_space=pltpu.SMEM),
            pl.BlockSpec((QB, HD), lambda h, i: (i, h)),
            pl.BlockSpec((k.shape[0], HD), lambda h, i: (0, h)),
            pl.BlockSpec((k.shape[0], HD), lambda h, i: (0, h)),
        ],
        out_specs=[
            pl.BlockSpec((QB, HD), lambda h, i: (i, h)),
            pl.BlockSpec((QB, HD), lambda h, i: (i, h)),
        ],
        compiler_params=pltpu.CompilerParams(vmem_limit_bytes=VMEM_LIMIT),
    )(chip, q, k, v)


def attend_back_kernel(chip_ref, q_ref, k_ref, v_ref, go_ref, lse_ref, gq_ref, gk_ref, gv_ref):
    i = pl.program_id(1)
    keys = pl.ds(pl.multiple_of(i * QB, QB), KB)
    base = (chip_ref[0] - 2) * 512 + i * QB
    q, k, v, go = q_ref[...], k_ref[keys, :], v_ref[keys, :], go_ref[...]
    scores = product(q, k, ((1,), (1,))) * SCALE
    scores = jnp.where(allowed_pairs(base), scores, MASKED)
    probs = jnp.exp(scores - lse_ref[:, :1])
    gp = product(go, v, ((1,), (1,)))
    inner = jnp.sum(probs * gp, axis=-1, keepdims=True)
    gs = (probs * (gp - inner)).astype(HALF)
    gq_ref[...] = (product(gs, k, ((1,), (0,))) * SCALE).astype(HALF)

    @pl.when(i == 0)
    def _():
        gk_ref[...] = jnp.zeros_like(gk_ref)
        gv_ref[...] = jnp.zeros_like(gv_ref)

    gk_ref[keys, :] += product(gs, q, ((0,), (0,))) * SCALE
    gv_ref[keys, :] += product(probs.astype(HALF), go, ((0,), (0,)))


def attend_back(chip, q, k, v, go, lse):
    tokens, width = q.shape
    heads = width // HD
    block = pl.BlockSpec((QB, HD), lambda h, i: (i, h))
    column = pl.BlockSpec((k.shape[0], HD), lambda h, i: (0, h))
    return pl.pallas_call(
        attend_back_kernel,
        out_shape=[
            jax.ShapeDtypeStruct((tokens, width), HALF),
            jax.ShapeDtypeStruct(k.shape, SINGLE),
            jax.ShapeDtypeStruct(k.shape, SINGLE),
        ],
        grid=(heads, tokens // QB),
        in_specs=[
            pl.BlockSpec(memory_space=pltpu.SMEM),
            block,
            column,
            column,
            block,
            block,
        ],
        out_specs=[block, column, column],
        compiler_params=pltpu.CompilerParams(vmem_limit_bytes=VMEM_LIMIT),
    )(chip, q, k, v, go, lse)


def halves(matrix):
    rows, width = matrix.shape
    padded = -(-width // 256) * 256
    matrix = jnp.pad(matrix, ((0, 0), (0, padded - width)))
    return jnp.moveaxis(matrix.reshape(rows, 2, padded // 2), 1, 0)


def whole(parts, width):
    return jnp.moveaxis(parts, 0, 1).reshape(parts.shape[1], -1)[:, :width]


def rms_scale(values, gain):
    inverse = lax.rsqrt(jnp.mean(values * values, axis=-1, keepdims=True) + EPSILON)
    return values * inverse * gain


def dot(a, b):
    return jnp.dot(a, b, preferred_element_type=SINGLE)


def dot_t(a, b):
    return product(a, b, ((1,), (1,)))


def t_dot(a, b):
    return product(a, b, ((0,), (0,)))


def per_device(
    hidden_in, attn_gain, w_query, w_key, w_value, w_out, ffn_gain, w_gate, w_up, w_down, out_grad
):
    features = hidden_in.shape[1]
    hidden_units = w_gate.shape[1]
    heads_width = w_query.shape[1] // 2
    chip = lax.div(lax.axis_index("seq"), 2)
    gains = jnp.pad(jnp.stack([attn_gain, ffn_gain], axis=1), ((0, 0), (0, 126)))
    gains = jnp.broadcast_to(gains, (2, *gains.shape))
    chunk_qkv = jnp.concatenate(
        [halves(w_query), halves(w_key), halves(w_value), gains], axis=2
    ).astype(HALF)
    chunk_out = halves(w_out.T).astype(HALF)
    chunk_ff = jnp.concatenate([halves(w_gate), halves(w_up)], axis=2).astype(HALF)
    chunk_down = halves(w_down.T).astype(HALF)
    ff = chunk_down.shape[-1]

    *gathered, earlier, own = gather_all(
        [chunk_qkv, chunk_out, chunk_ff, chunk_down], hidden_in, out_grad
    )
    w_qkv, wo_t, w_ff, wd_t = [w.reshape(features, w.shape[-1]) for w in gathered]
    gain_rows = w_qkv[:, 3 * heads_width :].T[:2].astype(SINGLE)
    gain_one, gain_two = gain_rows[:1], gain_rows[1:]
    w_qkv = w_qkv[:, : 3 * heads_width]
    own = own.reshape(2, 512, features)
    cot_full = own[1]
    rows = jnp.concatenate([earlier.reshape(1024, features), own[0]])

    first_in = rms_scale(rows.astype(SINGLE), gain_one).astype(HALF)
    first_own = first_in[1024:]
    queries = dot(first_own, w_qkv[:, :heads_width]).astype(HALF)
    kv = dot(first_in, w_qkv[:, heads_width:]).astype(HALF)
    keys, values = kv[:, :heads_width], kv[:, heads_width:]
    chip_ref = chip.reshape(1).astype(jnp.int32)
    attended, log_totals = attend(chip_ref, queries, keys, values)
    tokens = hidden_in.shape[0]
    rows_single = jax.ShapeDtypeStruct((tokens, features), SINGLE)
    rows_half = jax.ShapeDtypeStruct((tokens, features), HALF)
    mid, second_in = sum_call(
        post_mid, 1, dot_t(attended, wo_t), [hidden_in, gain_two], [rows_single], True
    )
    second_in = second_in.reshape(512, features)
    gate_up = dot(second_in, w_ff)
    gate, up_proj = gate_up[:, :ff], gate_up[:, ff:]
    hidden_ff = (jax.nn.silu(gate) * up_proj).astype(HALF)
    (hidden_out,) = sum_call(post_out, 2, dot_t(hidden_ff, wd_t), [mid], [rows_half], False)
    grad_hidden = dot(cot_full, wd_t)
    sig = jax.nn.sigmoid(gate)
    grad_gate = grad_hidden * up_proj * sig * (1.0 + gate * (1.0 - sig))
    grad_up = grad_hidden * gate * sig
    grad_ff = jnp.concatenate([grad_gate, grad_up], axis=1).astype(HALF)
    grad_mid, ffn_terms, grad_branch = sum_call(
        post_mid_back,
        3,
        dot_t(grad_ff, w_ff),
        [mid, out_grad, gain_two],
        [rows_single, rows_single],
        True,
    )
    grad_branch = grad_branch.reshape(512, features)
    grad_attended = dot(grad_branch, wo_t).astype(HALF)
    grad_q, grad_k, grad_v = attend_back(
        chip_ref, queries, keys, values, grad_attended, log_totals
    )
    grad_kv = jnp.concatenate([grad_k, grad_v], axis=1)
    grad_kv_own = return_call(
        grad_kv[1024:], grad_kv[:1024].astype(HALF).reshape(2, 512, 2 * heads_width)
    )
    grad_qkv = jnp.concatenate([grad_q, grad_kv_own], axis=1)
    in_grad, attn_terms = sum_call(
        post_in_back,
        4,
        dot_t(grad_qkv, w_qkv),
        [hidden_in, grad_mid, gain_one],
        [rows_single, rows_single],
        False,
    )
    terms = jnp.stack([attn_terms, ffn_terms]).reshape(2, tokens // ROWS, ROWS, features)
    gain_cols = jnp.pad(jnp.sum(terms[:, :, 0], axis=1).T, ((0, 0), (0, 126))).astype(HALF)
    g_down = t_dot(cot_full, hidden_ff).astype(HALF)
    g_ff = t_dot(second_in, grad_ff).astype(HALF)
    g_out = t_dot(grad_branch, attended).astype(HALF)
    g_qkv = t_dot(first_own, grad_qkv).astype(HALF)
    g_qkv = jnp.concatenate([g_qkv, gain_cols], axis=1)
    s_down, s_ff, s_out, s_qkv = scatter_all([g_down, g_ff, g_out, g_qkv])
    gain_sum = s_qkv[0, :, 3 * heads_width :] + s_qkv[1, :, 3 * heads_width :]
    h = heads_width
    return (
        hidden_out,
        in_grad,
        gain_sum[:, 0],
        whole(s_qkv[:, :, :h], 2 * h),
        whole(s_qkv[:, :, h : 2 * h], 2 * h),
        whole(s_qkv[:, :, 2 * h : 3 * h], 2 * h),
        whole(s_out, 2 * h).T,
        gain_sum[:, 1],
        whole(s_ff[:, :, :ff], hidden_units),
        whole(s_ff[:, :, ff:], hidden_units),
        whole(s_down, hidden_units).T,
    )


def solution(mesh):
    placed = (
        P("seq", None),
        P("seq"),
        P("seq", "tp"),
        P("seq", "tp"),
        P("seq", "tp"),
        P("tp", "seq"),
        P("seq"),
        P("seq", "tp"),
        P("seq", "tp"),
        P("tp", "seq"),
        P("seq", None),
    )
    return jax.shard_map(
        per_device,
        mesh=mesh,
        in_specs=placed,
        out_specs=(
            P("seq", None),
            P("seq", None),
            P("seq"),
            P("seq", "tp"),
            P("seq", "tp"),
            P("seq", "tp"),
            P("tp", "seq"),
            P("seq"),
            P("seq", "tp"),
            P("seq", "tp"),
            P("tp", "seq"),
        ),
        check_vma=False,
    )
```

time: 3470 us -> 752 us (0.22)
  waiting for transfers between devices: 2760 us -> 0 us
  Pallas kernels: 0 us -> 595 us
  blocking collectives: 416 us -> 0 us
  matrix products: 173 us -> 86.4 us
    reduce_scatter x7 -> x0, waiting for transfers between devices: 1870 us -> none  [the longest x1 323 us: per_device(): lax.psum_scatter(down_term, 'seq', scatter_dimension=1, tiled=True)]
    all_gather x7 -> x0, waiting for transfers between devices: 632 us -> none  [the longest x1 165 us: per_device(): lax.all_gather(w_query.astype(half), 'seq', axis=0, tiled=True)]
    pallas_call x0 -> x9, Pallas kernels: none -> 595 us  [the longest x1 222 us: gather_all(): pl.pallas_call(functools.partial(gather_kernel, n), out_shape=[jax.ShapeD...]
    unnamed x2 -> x0, blocking collectives: 416 us -> none
    psum x3 -> x0, waiting for transfers between devices: 225 us -> none  [pair_total(): return lax.psum(partial_value, 'tp')]
    dot_general x27 -> x13, matrix products: 173 us -> 86.4 us  [the longest x8 53.9 us: product(): lax.dot_general(a, b, (dims, ((), ())), preferred_element_type=SINGLE)]
  transfers between devices with their start and end apart: 25 -> 0, of which waited for: 20 -> 0; matrix products, arithmetic and copies ran while one was open for 5% -> 0% of each run, Pallas kernels for 0% -> 0%
where the time goes in v1:
time: 752 us; the launch traced here: 748 us
  Pallas kernels  595 us (79%)
  matrix products  86.4 us (11%)
  local copies, waits for them, and re-layouts  37.1 us (5%)
  other arithmetic  28.2 us (4%)
    pallas_call x1, Pallas kernels, gather_all(): pl.pallas_call(functools.partial(gather_kernel, n), out_shape=[jax.ShapeD...  222 us
    pallas_call x1, Pallas kernels, scatter_all(): pl.pallas_call(functools.partial(scatter_kernel, n), out_shape=[jax.Shape...  171 us
    pallas_call x4, Pallas kernels, sum_call(): pl.pallas_call(functools.partial(sum_kernel, post, len(ins), len(outs), s...  146 us
    dot_general x8, matrix products, product(): lax.dot_general(a, b, (dims, ((), ())), preferred_element_type=SINGLE)  53.9 us
    dot_general x5, matrix products, dot(): return jnp.dot(a, b, preferred_element_type=SINGLE)  32.5 us
    pallas_call x1, Pallas kernels, return_call(): pl.pallas_call(return_kernel, out_shape=jax.ShapeDtypeStruct(own.shape, H...  30.2 us
    pallas_call x1, Pallas kernels, attend_back(): pl.pallas_call(attend_back_kernel, out_shape=[jax.ShapeDtypeStruct((token...  15.9 us

profile of v1, /device:TPU:1, one launch (start us, length us, event | category | flops | bytes accessed | tf_op | source)
XLA Modules:
  0.0 748.2 jit_solution(12422575293135614536)
XLA Ops:
  10.1 221.5 %shard_map.194 = (bf16[4,2,4,2,32,1664]{5,4,3,2,1,0:T(8,128)(2,1)}, bf16[4,2,4,2,32,512]{5,4,3,2,1,0:T(8,128)(2,1)}, bf16[4,2,4,2,32,2816]{5,4,3,2,1,0:T(8,128)(...) custom-call(bf16[2,32,1664]{2,1,0:T(8,128)(2,1)} %pad_maximum_fusion, ...), custom_call_target="tpu_custom_call" | custom-call | tf_op jit(solution)/shard_map/pallas_call | solution.py:261
  233.6 4.1 fusion.33
  241.1 8.2 %fusion.3 = bf16[1536,2048]{1,0:T(8,128)(2,1)S(1)} fusion(f32[2048]{0:T(1024)S(1)} %bitcast.171, f32[1536]{0:T(1024)S(1)} %add_rsqrt_fusion, bf16[512,2048]{1,0:T(8,128)(2,1)S(1)} %bitcast.134, bf16[1024,2048]{1,0:T(8,128)(2,1)S(1)} %bitcast.136), kind=kLoop, calls=%fused_computation.6 | loop fusion | flops 22020096 | bytes 12597248 | tf_op jit(solution)/shard_map/convert_element_type | solution.py:785
  252.1 7.1 fusion.9
  261.1 10.6 %shard_map.195 = (bf16[512,512]{1,0:T(8,128)(2,1)}, f32[512,512]{1,0:T(8,128)}) custom-call(s32[1]{0:T(128)} %bitcast.chip_ref, bf16[512,512]{1,0:T(8,128)(2,1)} %fusion.23.q_ref, bf16[1536,512]{1,0:T(8,128)(2,1)} %get-tuple-element.63.k_ref, bf16[1536,512]{1,0:T(8,128)(2,1)} %get-tuple-element.62.v_ref), custom_call_target="tpu_custom_call" | custom-call | tf_op jit(solution)/shard_map/pallas_call | solution.py:660
  271.7 4.3 fusion.36.refs_0_
  275.9 43.0 %shard_map.196 = (f32[256,2048]{1,0:T(8,128)}, bf16[2,256,2048]{2,1,0:T(8,128)(2,1)}) custom-call(f32[2,256,2048]{2,1,0:T(8,128)} %fusion.36.refs_0_, bf16[256,2048]{1,0:T(8,128)(2,1)} %refs_1_.3, f32[1,2048]{1,0:T(1,128)} %get-tuple-element.69.refs_2_.refs_3_), custom_call_target="tpu_custom_call" | custom-call | tf_op jit(solution)/shard_map/pallas_call | solution.py:533
  319.0 10.3 %fusion.37 = f32[512,2816]{1,0:T(8,128)S(1)} fusion(bf16[512,2048]{1,0:T(8,128)(2,1)} %bitcast.187, bf16[2048,2816]{1,0:T(8,128)(2,1)} %bitcast.179), kind=kOutput, calls=%fused_computation.73 | convolution fusion | flops 5905580032 | bytes 19398656 | tf_op jit(solution)/shard_map/dot_general | solution.py:746
  329.3 8.7 %multiply_convert_fusion.1 = (bf16[512,1408]{1,0:T(8,128)(2,1)S(1)}, bf16[512,1408]{1,0:T(8,128)(2,1)}, bf16[512,1408]{1,0:T(8,128)(2,1)}) fusion(f32[512,2816]{1,0:T(8,128)S(1)} %fusion.37, bf16[512,2048]{1,0:T(8,128)(2,1)S(1)} %bitcast.148, bf16[2048,1408]{1,0:T(8,128)(2,1)} %bitcast.183), kind=kOutput, calls=%fused_computation.27 | convolution fusion | flops 2964324352 | bytes 17956864 | tf_op jit(solution)/shard_map/dot_general | solution.py:746
  338.1 8.9 %fusion.12.refs_0_ = f32[2,256,2048]{2,1,0:T(8,128)} fusion(bf16[2048,2816,1]{1,0,2:T(8,128)(2,1)S(1)} %bitcast.182, bf16[2,256,1408]{2,1,0:T(8,128)(2,1)} %bitcast.194, bf16[2,256,1408]{2,1,0:T(8,128)(2,1)S(1)} %bitcast.193), kind=kOutput, calls=%fused_computation.19 | convolution fusion | flops 5911347200 | bytes 18612224 | tf_op jit(solution)/shard_map/dot_general | solution.py:640
  347.0 6.5 fusion.38.refs_0_
  353.6 32.1 %shard_map.197 = bf16[256,2048]{1,0:T(8,128)(2,1)} custom-call(f32[2,256,2048]{2,1,0:T(8,128)} %fusion.38.refs_0_, f32[256,2048]{1,0:T(8,128)} %get-tuple-element.41.refs_1_), custom_call_target="tpu_custom_call" | custom-call | tf_op jit(solution)/shard_map/pallas_call | solution.py:533
  385.7 36.2 %shard_map.198 = (f32[256,2048]{1,0:T(8,128)}, f32[256,2048]{1,0:T(8,128)}, bf16[2,256,2048]{2,1,0:T(8,128)(2,1)}) custom-call(f32[2,256,2048]{2,1,0:T(8,128)} %fusion.12.refs_0_, f32[256,2048]{1,0:T(8,128)} %get-tuple-element.41.refs_1_, bf16[256,2048]{1,0:T(8,128)(2,1)} %refs_2_.1, f32[1,2048]{1,0:T(1,128)} %get-tuple-element.69.refs_2_.refs_3_), custom_call_target="tpu_custom_call" | custom-call | tf_op jit(solution)/shard_map/pallas_call | solution.py:533
  422.0 3.8 convolution_convert_fusion.4.go_ref
  428.4 15.9 %shard_map.199 = (bf16[512,512]{1,0:T(8,128)(2,1)}, f32[1536,512]{1,0:T(8,128)}, f32[1536,512]{1,0:T(8,128)}) custom-call(s32[1]{0:T(128)} %bitcast.chip_ref, bf16[512,512]{1,0:T(8,128)(2,1)} %fusion.23.q_ref, bf16[1536,512]{1,0:T(8,128)(2,1)} %get-tuple-element.63.k_ref, bf16[1536,512]{1,0:T(8,128)(2,1)} %get-tuple-element.62.v_ref, ...), custom_call_target="tpu_custom_call" | custom-call | tf_op jit(solution)/shard_map/pallas_call | solution.py:708
  450.6 30.2 %shard_map.200 = bf16[512,1024]{1,0:T(8,128)(2,1)} custom-call(f32[512,1024]{1,0:T(8,128)} %slice.132.own, bf16[2,512,1024]{2,1,0:T(8,128)(2,1)} %bitcast.139), custom_call_target="tpu_custom_call" | custom-call | tf_op jit(solution)/shard_map/pallas_call | solution.py:612
  480.9 8.6 %fusion.5 = f32[512,2048]{1,0:T(8,128)} fusion(bf16[2048,1664]{1,0:T(8,128)(2,1)} %bitcast.173, bf16[512,1024]{1,0:T(8,128)(2,1)} %shard_map.200, bf16[512,512]{1,0:T(8,128)(2,1)S(1)} %copy-done.16), kind=kOutput, calls=%fused_computation.11 | convolution fusion | flops 3224371200 | bytes 12058624 | tf_op jit(solution)/shard_map/dot_general | solution.py:640
  489.5 7.1 convolution_convert_fusion.1
  496.5 35.0 %shard_map.201 = (f32[256,2048]{1,0:T(8,128)}, f32[256,2048]{1,0:T(8,128)}) custom-call(f32[2,256,2048]{2,1,0:T(8,128)} %bitcast.141, bf16[256,2048]{1,0:T(8,128)(2,1)} %refs_1_.3, f32[256,2048]{1,0:T(8,128)} %get-tuple-element.47.refs_2_, f32[1,2048]{1,0:T(1,128)} %copy-done.13), custom_call_target="tpu_custom_call" | custom-call | tf_op jit(solution)/shard_map/pallas_call | solution.py:533
  532.9 6.7 fusion.4
  539.7 9.9 %copy.69 = bf16[2048,1664]{1,0:T(8,128)(2,1)} copy(bf16[2048,1664]{0,1:T(8,128)(2,1)} %fusion.4) | data formatting | bytes 13631488 | tf_op jit(solution)/shard_map/concatenate | solution.py:840
  549.5 6.8 convolution_convert_fusion.2
  556.3 9.0 %convolution_convert_fusion = bf16[2048,2816]{1,0:T(8,128)(2,1)} fusion(bf16[512,2048]{1,0:T(8,128)(2,1)S(1)} %bitcast.188, bf16[512,1408]{1,0:T(8,128)(2,1)S(1)} %copy-done.17, bf16[512,1408]{1,0:T(8,128)(2,1)S(1)} %get-tuple-element.57), kind=kOutput, calls=%fused_computation.7 | convolution fusion | flops 5917114368 | bytes 16515072 | tf_op jit(solution)/shard_map/dot_general | solution.py:640
  565.4 170.6 %shard_map.202 = (f32[2,32,1408]{2,1,0:T(8,128)}, f32[2,32,2816]{2,1,0:T(8,128)}, f32[2,32,512]{2,1,0:T(8,128)}, f32[2,32,1664]{2,1,0:T(8,128)}) custom-call(bf16[4,2,4,2,32,1408]{5,4,3,2,1,0:T(8,128)(2,1)} %bitcast.140, bf16[4,2,4,2,32,2816]{5,4,3,2,1,0:T(8,128)(2,1)} %bitcast.137, bf16[4,2,4,2,32,512]{5,4,3,2,1,0:T(8,128)(2,1)} %bitcast.143, ...), custom_call_target="tpu_custom_call" | custom-call | tf_op jit(solution)/shard_map/pallas_call | solution.py:448
  (102 shorter events, 41.6 us)
Async XLA Ops:
  0.6 8.7 %copy-start.12 = (f32[2752,32]{0,1:T(8,128)S(1)}, f32[2752,32]{0,1:T(8,128)}, u32[]{:S(2)}) copy-start(f32[2752,32]{0,1:T(8,128)} %param.20) | copy-start | bytes 1056772
  233.6 7.5 %copy-start.13 = (f32[1,2048]{1,0:T(1,128)}, f32[1,2048]{1,0:T(1,128)S(1)}, u32[]{:S(2)}) copy-start(f32[1,2048]{1,0:T(1,128)S(1)} %get-tuple-element.70.refs_3_) | copy-start | bytes 24580
  233.6 4.1 copy-start
  237.7 11.6 %slice-start = ((s8[6815744]{0:T(1024)(128)(4,1)}), s8[4194304]{0:T(1024)(128)(4,1)S(1)}, s32[]{:S(2)}) async-start(s8[6815744]{0:T(1024)(128)(4,1)} %bitcast.174), calls=%async_computation | async-start | bytes 8388608
  241.1 8.2 %slice-start.1 = ((s8[6815744]{0:T(1024)(128)(4,1)}), s8[2621440]{0:T(1024)(128)(4,1)S(1)}, s32[]{:S(2)}) async-start(s8[6815744]{0:T(1024)(128)(4,1)} %bitcast.174), calls=%async_computation.1 | async-start | bytes 5242880
  261.1 10.6 %copy-start.4 = (bf16[4,2,4,2,32,512]{5,4,3,2,1,0:T(8,128)(2,1)S(1)}, bf16[4,2,4,2,32,512]{5,4,3,2,1,0:T(8,128)(2,1)}, u32[]{:S(2)}) copy-start(bf16[4,2,4,2,32,512]{5,4,3,2,1,0:T(8,128)(2,1)} %get-tuple-element.37) | copy-start | bytes 6291460
  319.0 10.3 %copy-start.7 = (bf16[1,2,2,128,2048]{4,3,2,1,0:T(8,128)(2,1)S(1)}, bf16[1,2,2,128,2048]{4,3,2,1,0:T(8,128)(2,1)}, u32[]{:S(2)}) copy-start(bf16[1,2,2,128,2048]{4,3,2,1,0:T(8,128)(2,1)} %get-tuple-element.60) | copy-start | bytes 6291460
  319.0 19.1 %slice-start.2 = ((s8[11534336]{0:T(1024)(128)(4,1)}), s8[4194304]{0:T(1024)(128)(4,1)S(1)}, s32[]{:S(2)}) async-start(s8[11534336]{0:T(1024)(128)(4,1)} %bitcast.180), calls=%async_computation.2 | async-start | bytes 8388608
  319.0 19.1 %slice-start.3 = ((s8[11534336]{0:T(1024)(128)(4,1)}), s8[4194304]{0:T(1024)(128)(4,1)S(1)}, s32[]{:S(2)}) async-start(s8[11534336]{0:T(1024)(128)(4,1)} %bitcast.180), calls=%async_computation.3 | async-start | bytes 8388608
  329.3 8.8 %slice-start.4 = ((s8[11534336]{0:T(1024)(128)(4,1)}), s8[3145728]{0:T(1024)(128)(4,1)S(1)}, s32[]{:S(2)}) async-start(s8[11534336]{0:T(1024)(128)(4,1)} %bitcast.180), calls=%async_computation.4 | async-start | bytes 6291456
  329.3 17.7 %slice-start.5 = ((s8[5767168]{0:T(1024)(128)(4,1)}), s8[4194304]{0:T(1024)(128)(4,1)S(1)}, s32[]{:S(2)}) async-start(s8[5767168]{0:T(1024)(128)(4,1)} %bitcast.184), calls=%async_computation.5 | async-start | bytes 8388608
  338.1 8.9 %slice-start.6 = ((s8[5767168]{0:T(1024)(128)(4,1)}), s8[1572864]{0:T(1024)(128)(4,1)S(1)}, s32[]{:S(2)}) async-start(s8[5767168]{0:T(1024)(128)(4,1)} %bitcast.184), calls=%async_computation.6 | async-start | bytes 3145728
  421.9 3.8 copy-start.11
  422.0 3.8 copy-start.15
  444.3 2.8 copy-start.3
  450.6 30.2 %copy-start.16 = (bf16[512,512]{1,0:T(8,128)(2,1)S(1)}, bf16[512,512]{1,0:T(8,128)(2,1)}, u32[]{:S(2)}) copy-start(bf16[512,512]{1,0:T(8,128)(2,1)} %get-tuple-element.44) | copy-start | bytes 1572868
  480.8 8.6 %copy-start.9 = (bf16[512,1024]{1,0:T(8,128)(2,1)S(1)}, bf16[512,1024]{1,0:T(8,128)(2,1)}, u32[]{:S(2)}) copy-start(bf16[512,1024]{1,0:T(8,128)(2,1)} %shard_map.200) | copy-start | bytes 3145732
  496.5 35.0 %copy-start.6 = (f32[256,2048]{1,0:T(8,128)S(1)}, f32[256,2048]{1,0:T(8,128)}, u32[]{:S(2)}) copy-start(f32[256,2048]{1,0:T(8,128)} %get-tuple-element.50) | copy-start | bytes 6291460
  539.7 9.9 %copy-start.8 = (bf16[1,2,2,128,2048]{4,3,2,1,0:T(8,128)(2,1)S(1)}, bf16[1,2,2,128,2048]{4,3,2,1,0:T(8,128)(2,1)}, u32[]{:S(2)}) copy-start(bf16[1,2,2,128,2048]{4,3,2,1,0:T(8,128)(2,1)} %get-tuple-element.60) | copy-start | bytes 6291460
  549.5 6.8 copy-start.14
  549.5 6.8 copy-start.17
  736.0 8.1 %copy-start.10 = (f32[2,32,2816]{2,1,0:T(8,128)S(1)}, f32[2,32,2816]{2,1,0:T(8,128)}, u32[]{:S(2)}) copy-start(f32[2,32,2816]{2,1,0:T(8,128)} %get-tuple-element.53) | copy-start | bytes 2162692
  736.0 9.7 %copy-start.2 = (bf16[256,2048]{1,0:T(8,128)(2,1)S(1)}, bf16[256,2048]{1,0:T(8,128)(2,1)}, u32[]{:S(2)}) copy-start(bf16[256,2048]{1,0:T(8,128)(2,1)} %shard_map.197) | copy-start | bytes 3145732
  742.2 4.5 copy-start.5
  (1 other events, 2.8 us)

commit v2 on v1

--- a/solution.py
+++ b/solution.py
@@ -151,58 +151,6 @@
     return [step0, step1, step2, step3, step4, step5, step6]
 
 
-def halo_steps(hid, cot, xh, cots, sems, local_sems):
-    x, y, z, c, t = coords()
-    core = device(x, y, z, 1 - c, t)
-    pair = device(x, y, z, c, 1 - t)
-    locals_ = [
-        pltpu.make_async_copy(hid, cots.at[0, c], local_sems.at[0]),
-        pltpu.make_async_copy(cot, cots.at[1, c], local_sems.at[1]),
-    ]
-    swaps = [
-        sems.copy(hid, cots.at[0, c], core),
-        sems.copy(cot, cots.at[1, c], core),
-    ]
-    parts = []
-    for j, shift in ((1, 1), (0, 2)):
-        slot, other = xh.at[j, c, t], xh.at[j, c, 1 - t]
-        parts.append(
-            dict(
-                first=sems.copy(hid.at[t], slot, chip_shift(shift)),
-                pair=sems.copy(slot, slot, pair),
-                core=sems.copy(slot, slot, core),
-                both=sems.copy(other, other, core),
-            )
-        )
-
-    def step0():
-        for copy in locals_:
-            copy.start()
-        sems.start(*[p["first"] for p in parts])
-        sems.start(*swaps)
-
-    def step1():
-        for p in parts:
-            p["first"].wait_recv()
-            sems.start(p["pair"], p["core"])
-
-    def step2():
-        for p in parts:
-            p["pair"].wait_recv()
-            sems.start(p["both"])
-
-    def step3():
-        for p in parts:
-            p["core"].wait_recv()
-            p["both"].wait_recv()
-        for copy in locals_:
-            copy.wait()
-        for copy in swaps:
-            copy.wait_recv()
-
-    return [step0, step1, step2, step3]
-
-
 def neighbours():
     x, y, z, c, t = coords()
     return [
@@ -215,67 +163,314 @@
     ]
 
 
-def gather_kernel(chunks, *refs):
-    w_in, (hid, cot) = refs[:chunks], refs[chunks : chunks + 2]
-    rest = refs[chunks + 2 :]
-    w_out, (xh, cots) = rest[:chunks], rest[chunks : chunks + 2]
-    send, recv, local_sems = rest[chunks + 2 :]
+def product(a, b, dims):
+    return lax.dot_general(a, b, (dims, ((), ())), preferred_element_type=SINGLE)
+
+
+QB = 256
+KB = QB + WINDOW
+SCALE = 1.0 / math.sqrt(HD)
+PARTS = 2
+ROWS = 16
+LANES = 128
+
+
+def allowed_pairs(base):
+    row = lax.broadcasted_iota(jnp.int32, (QB, KB), 0)
+    col = lax.broadcasted_iota(jnp.int32, (QB, KB), 1)
+    return (col > row) & (col <= row + WINDOW) & (col + base >= 0)
+
+
+def attend_block(q, k, v, base):
+    scores = product(q, k, ((1,), (1,))) * SCALE
+    scores = jnp.where(allowed_pairs(base), scores, MASKED)
+    row_max = jnp.max(scores, axis=-1, keepdims=True)
+    expon = jnp.exp(scores - row_max)
+    row_total = jnp.sum(expon, axis=-1, keepdims=True)
+    probs = (expon * (1.0 / row_total)).astype(HALF)
+    mixed = product(probs, v, ((1,), (0,))).astype(HALF)
+    return mixed, row_max + jnp.log(row_total)
+
+
+def rms_inverse(values):
+    return lax.rsqrt(jnp.mean(values * values, axis=-1, keepdims=True) + EPSILON)
+
+
+def row_loop(start, count, fn, step=ROWS):
+    def body(i, carry):
+        fn(pl.ds(pl.multiple_of(start + i * step, step), step))
+        return carry
+
+    lax.fori_loop(0, count // step, body, 0)
+
+
+def columns(w, n, size):
+    return w[:, :, :, :, :, pl.ds(n, size)].reshape(2048, size)
+
+
+CHUNK_QKV, CHUNK_OUT, CHUNK_FF, CHUNK_DOWN = range(4)
+GATHER_TIMES = (-4.0, -3.0, -2.0, -1.1, 0.0, 0.6, 1.5)
+
+
+def forward_kernel(*refs):
+    w_in, (hid, cot) = refs[:4], refs[4:6]
+    w_out = refs[6:10]
+    a1, cots, q, kv, o, lse, mid, a2, hid_ff, grad_ff, gains = refs[10:21]
+    (
+        rows,
+        w_qkv,
+        w_o,
+        w_ff,
+        cot_v,
+        gate_up,
+        to_core,
+        from_core,
+        to_pair,
+        from_pair,
+        send,
+        recv,
+        local_sems,
+    ) = refs[21:]
     x, y, z, c, t = coords()
+    chip = lax.div(lax.axis_index("seq"), 2)
+    core, pair = device(x, y, z, 1 - c, t), device(x, y, z, c, 1 - t)
     sems = Sems(send, recv)
-    greet(
-        neighbours()
-        + [device(x, y, z, c, 1 - t), chip_shift(1), chip_shift(-1), chip_shift(2), chip_shift(-2)]
+    greet(neighbours() + [pair, chip_shift(1), chip_shift(-1), chip_shift(2), chip_shift(-2)])
+
+    chunk_steps = [gather_steps(w_in[i], w_out[i], sems, local_sems.at[i]) for i in range(4)]
+    order = sorted(
+        (i + GATHER_TIMES[j], i, j) for i in range(4) for j in range(1, len(GATHER_TIMES))
     )
-    halo = halo_steps(hid, cot, xh, cots, sems, local_sems)
-    chunk_steps = [
-        gather_steps(w_in[i], w_out[i], sems, local_sems.at[2 + i]) for i in range(chunks)
-    ]
-    halo[0]()
     for steps in chunk_steps:
         steps[0]()
-    for steps in chunk_steps:
-        steps[1]()
-    order = []
-    for i in range(chunks):
-        for j in range(2, 7):
-            order.append((2 * i + j, i, j))
-    done_halo = 1
-    for tick in sorted({o[0] for o in order}):
-        for when, i, j in sorted(order):
-            if when == tick:
-                chunk_steps[i][j]()
-        if tick >= 4 and done_halo < 4:
-            halo[done_halo]()
-            done_halo += 1
-    while done_halo < 4:
-        halo[done_halo]()
-        done_halo += 1
+
+    def pump(count=1):
+        for _ in range(min(count, len(order))):
+            _, i, j = order.pop(0)
+            chunk_steps[i][j]()
+
+    def pump_until(chunk):
+        while any(i == chunk for _, i, _ in order):
+            pump()
+
+    row_copy = pltpu.make_async_copy(hid, rows.at[c], local_sems.at[4])
+    cot_copy = pltpu.make_async_copy(cot, cots.at[c], local_sems.at[5])
+    row_swap = sems.copy(hid, rows.at[c], core)
+    cot_swap = sems.copy(cot, cots.at[c], core)
+    row_copy.start()
+    cot_copy.start()
+    sems.start(row_swap, cot_swap)
+
+    def load(chunk, target, sem):
+        copy = pltpu.make_async_copy(w_out[chunk], target, local_sems.at[sem])
+        copy.start()
+        return copy
+
+    pump_until(CHUNK_QKV)
+    load_qkv = load(CHUNK_QKV, w_qkv, 6)
+    row_copy.wait()
+    row_swap.wait_recv()
+    load_qkv.wait()
+    pick = (
+        lax.broadcasted_iota(jnp.int32, (8, LANES), 0)
+        == lax.broadcasted_iota(jnp.int32, (8, LANES), 1)
+    ).astype(HALF)
+    gains[...] = product(pick, columns(w_qkv, 1536, LANES), ((1,), (1,)))
+
+    for half in range(2):
+
+        def norm_one(r, half=half):
+            values = rows[half, r, :].astype(SINGLE)
+            normed = values * rms_inverse(values) * gains[0:1, :]
+            a1[half, r, :] = normed.astype(HALF)
+
+        row_loop(0, 256, norm_one)
+    pump()
+
+    def project(n):
+        return [product(a1[half], columns(w_qkv, n, 256), ((1,), (0,))).astype(HALF) for half in range(2)]
+
+    def project_kv(i, carry):
+        n = pl.multiple_of(i * 256, 256)
+        out = project(512 + n)
+        for half in range(2):
+            kv[1024 + half * 256 : 1280 + half * 256, pl.ds(n, 256)] = out[half]
+        return carry
+
+    lax.fori_loop(0, 4, project_kv, 0)
+    own_kv = kv.at[1024:1536]
+    halo = [
+        sems.copy(own_kv, kv.at[512:1024], chip_shift(1)),
+        sems.copy(own_kv, kv.at[0:512], chip_shift(2)),
+    ]
+    sems.start(*halo)
+    pump()
+
+    def project_q(i, carry):
+        n = pl.multiple_of(i * 256, 256)
+        out = project(n)
+        for half in range(2):
+            q[half * 256 : 256 + half * 256, pl.ds(n, 256)] = out[half]
+        return carry
+
+    lax.fori_loop(0, 2, project_q, 0)
+    pump_until(CHUNK_OUT)
+    load_o = load(CHUNK_OUT, w_o, 7)
+    for copy in halo:
+        copy.wait_recv()
+    for h in range(4):
+        head = slice(h * HD, (h + 1) * HD)
+        value_head = slice(512 + h * HD, 512 + (h + 1) * HD)
+
+        def attend_one(i, carry, head=head, value_head=value_head):
+            mine = pl.ds(pl.multiple_of(i * QB, QB), QB)
+            keys = pl.ds(pl.multiple_of(i * QB, QB), KB)
+            base = (chip - 2) * 512 + i * QB
+            mixed, total = attend_block(q[mine, head], kv[keys, head], kv[keys, value_head], base)
+            o[mine, head] = mixed
+            lse[mine, head] = jnp.broadcast_to(total, (QB, HD))
+            return carry
+
+        lax.fori_loop(0, 2, attend_one, 0)
+        pump()
+    load_o.wait()
+
+    size = 256 // PARTS
+    parts = [pl.ds(i * size, size) for i in range(PARTS)]
+
+    def out_rows(start):
+        def tile(n):
+            w_rows = w_o[n].reshape(512, 512)
+            return product(o[pl.ds(start, size), :], w_rows, ((1,), (1,)))
+
+        return tile
+
+    core_copies = [sems.copy(to_core.at[r], from_core.at[r], core) for r in parts]
+    pair_copies = [sems.copy(to_pair.at[r], from_pair.at[r], pair) for r in parts]
+    for i in range(PARTS):
+        tile = out_rows(pl.multiple_of((1 - c) * 256 + i * size, size))
+        for n in range(4):
+            to_core[parts[i], n * 512 : (n + 1) * 512] = tile(n).astype(HALF)
+        sems.start(core_copies[i])
+    for i in range(PARTS):
+        tile = out_rows(pl.multiple_of(c * 256 + i * size, size))
+        core_copies[i].wait_recv()
+        for n in range(4):
+            cols = slice(n * 512, (n + 1) * 512)
+            to_pair[parts[i], cols] = (
+                tile(n) + from_core[parts[i], cols].astype(SINGLE)
+            ).astype(HALF)
+        sems.start(pair_copies[i])
+    pump()
+    spreads = []
+    for i in range(PARTS):
+        pair_copies[i].wait_recv()
+
+        def norm_two(r):
+            total = to_pair[r, :].astype(SINGLE) + from_pair[r, :].astype(SINGLE)
+            values = rows[c, r, :].astype(SINGLE) + total
+            mid[r, :] = values
+            a2[c, r, :] = (values * rms_inverse(values) * gains[1:2, :]).astype(HALF)
+
+        row_loop(i * size, size, norm_two)
+        copy = sems.copy(a2.at[c, parts[i]], a2.at[c, parts[i]], core)
+        sems.start(copy)
+        spreads.append(copy)
+    pump_until(CHUNK_FF)
+    load_ff = load(CHUNK_FF, w_ff, 8)
+    for copy in spreads:
+        copy.wait_recv()
+    load_ff.wait()
+
+    def gate_and_up(i, carry):
+        n = pl.multiple_of(i * 2 * LANES, 2 * LANES)
+        w_cols = columns(w_ff, n, 2 * LANES)
+        for half in range(2):
+            r = slice(half * 256, (half + 1) * 256)
+            both = product(a2[half], w_cols, ((1,), (0,)))
+            gate_up[r, pl.ds(n, 2 * LANES)] = both
+            gate, up_part = both[:, :LANES], both[:, LANES:]
+            hid_part = gate / (1.0 + jnp.exp(-gate)) * up_part
+            hid_ff[r, pl.ds(pl.multiple_of(i * LANES, LANES), LANES)] = hid_part.astype(HALF)
+        return carry
+
+    lax.fori_loop(0, 11, gate_and_up, 0)
+    pump(len(order))
+    load_down = pltpu.make_async_copy(
+        w_out[CHUNK_DOWN], w_qkv.at[:, :, :, :, :, 0:1408], local_sems.at[9]
+    )
+    load_down.start()
+    cot_copy.wait()
+    cot_swap.wait_recv()
+    load_cot = pltpu.make_async_copy(cots, cot_v, local_sems.at[10])
+    load_cot.start()
+    load_cot.wait()
+    load_down.wait()
+
+    def back(i, carry):
+        n = pl.multiple_of(i * LANES, LANES)
+        w_cols = columns(w_qkv, n, LANES)
+        n2 = pl.multiple_of(i * 2 * LANES, LANES)
+        for half in range(2):
+            r = slice(half * 256, (half + 1) * 256)
+            ghid = product(cot_v[half], w_cols, ((1,), (0,)))
+            gate = gate_up[r, pl.ds(n2, LANES)]
+            up_part = gate_up[r, pl.ds(n2 + LANES, LANES)]
+            sig = 1.0 / (1.0 + jnp.exp(-gate))
+            grad_ff[r, pl.ds(n2, LANES)] = (
+                ghid * up_part * sig * (1.0 + gate * (1.0 - sig))
+            ).astype(HALF)
+            grad_ff[r, pl.ds(n2 + LANES, LANES)] = (ghid * gate * sig).astype(HALF)
+        return carry
+
+    lax.fori_loop(0, 11, back, 0)
     sems.finish()
 
 
-def gather_all(chunks, hid, cot):
-    n = len(chunks)
+def forward(chunks, hid, cot):
     features = hid.shape[-1]
     anywhere = pl.BlockSpec(memory_space=pl.ANY)
-    copies = 19 * n + 10
+    in_vmem = pl.BlockSpec(memory_space=pltpu.VMEM)
+    copies = 19 * 4 + 4 + 3 * PARTS
+    shape = jax.ShapeDtypeStruct
+    ff = chunks[CHUNK_DOWN].shape[-1]
+    full = lambda w: (4, 2, 4, 2, 32, w)
     return pl.pallas_call(
-        functools.partial(gather_kernel, n),
-        out_shape=[jax.ShapeDtypeStruct((4, 2, 4, 2, 32, w.shape[-1]), HALF) for w in chunks]
+        forward_kernel,
+        out_shape=[shape(full(w.shape[-1]), HALF) for w in chunks]
         + [
-            jax.ShapeDtypeStruct((2, 2, 2, 128, features), HALF),
-            jax.ShapeDtypeStruct((2, 2, 2, 128, features), HALF),
+            shape((2, 256, features), HALF),
+            shape((2, 256, features), HALF),
+            shape((512, 512), HALF),
+            shape((1536, 1024), HALF),
+            shape((512, 512), HALF),
+            shape((512, 512), SINGLE),
+            shape((256, features), SINGLE),
+            shape((2, 256, features), HALF),
+            shape((512, ff), HALF),
+            shape((512, 2 * ff), HALF),
+            shape((8, features), SINGLE),
         ],
-        in_specs=[anywhere] * (n + 2),
-        out_specs=[anywhere] * (n + 2),
+        in_specs=[anywhere] * 6,
+        out_specs=[anywhere] * 4 + [in_vmem, anywhere] + [in_vmem] * 9,
         scratch_shapes=[
+            pltpu.VMEM((2, 256, features), HALF),
+            pltpu.VMEM(full(chunks[CHUNK_QKV].shape[-1]), HALF),
+            pltpu.VMEM((4, 2, 4, 2, 32, 512), HALF),
+            pltpu.VMEM(full(2 * ff), HALF),
+            pltpu.VMEM((2, 256, features), HALF),
+            pltpu.VMEM((512, 2 * ff), SINGLE),
+        ]
+        + [pltpu.VMEM((256, features), HALF) for _ in range(4)]
+        + [
             pltpu.SemaphoreType.DMA((copies,)),
             pltpu.SemaphoreType.DMA((copies,)),
-            pltpu.SemaphoreType.DMA((2 + n,)),
+            pltpu.SemaphoreType.DMA((11,)),
         ],
         compiler_params=pltpu.CompilerParams(
             collective_id=0, has_side_effects=True, vmem_limit_bytes=VMEM_LIMIT
         ),
-    )(*chunks, hid.reshape(2, 128, features), cot.reshape(2, 128, features))
+    )(*chunks, hid, cot)
 
 
 def add_blocks(target, index, sources):
@@ -463,10 +658,6 @@
     )(*[g.reshape(4, 2, 4, 2, 32, g.shape[-1]) for g in chunks])
 
 
-PARTS = 4
-ROWS = 16
-
-
 def sum_kernel(post, n_in, n_out, spread, *refs):
     part, ins = refs[0], refs[1 : 1 + n_in]
     outs = refs[1 + n_in : 1 + n_in + n_out]
@@ -543,15 +734,6 @@
     )(part.reshape(2, tokens, features), *ins)
 
 
-def post_mid(r, total, ins, outs):
-    hidden, gain = ins
-    (mid_out,) = outs
-    mid = hidden[r, :].astype(SINGLE) + total
-    mid_out[r, :] = mid
-    inverse = lax.rsqrt(jnp.mean(mid * mid, axis=-1, keepdims=True) + EPSILON)
-    return mid * inverse * gain[...]
-
-
 def post_out(r, total, ins, outs):
     outs[0][r, :] = (ins[0][r, :] + total).astype(HALF)
 
@@ -562,10 +744,6 @@
     slope = jnp.mean(scaled * values, axis=-1, keepdims=True)
     gain_term = jnp.sum(grad * values * inverse, axis=0, keepdims=True)
     return inverse * scaled - values * (inverse * inverse * inverse * slope), gain_term
-
-
-def add_gain_term(gain_out, r, term):
-    gain_out[...] += term
 
 
 def post_mid_back(r, total, ins, outs):
@@ -623,59 +801,6 @@
             collective_id=5, has_side_effects=True, vmem_limit_bytes=VMEM_LIMIT
         ),
     )(own, far)
-
-
-QB = 256
-KB = QB + WINDOW
-SCALE = 1.0 / math.sqrt(HD)
-
-
-def allowed_pairs(base):
-    row = lax.broadcasted_iota(jnp.int32, (QB, KB), 0)
-    col = lax.broadcasted_iota(jnp.int32, (QB, KB), 1)
-    return (col > row) & (col <= row + WINDOW) & (col + base >= 0)
-
-
-def product(a, b, dims):
-    return lax.dot_general(a, b, (dims, ((), ())), preferred_element_type=SINGLE)
-
-
-def attend_kernel(chip_ref, q_ref, k_ref, v_ref, o_ref, lse_ref):
-    i = pl.program_id(1)
-    keys = pl.ds(pl.multiple_of(i * QB, QB), KB)
-    base = (chip_ref[0] - 2) * 512 + i * QB
-    scores = product(q_ref[...], k_ref[keys, :], ((1,), (1,))) * SCALE
-    scores = jnp.where(allowed_pairs(base), scores, MASKED)
-    row_max = jnp.max(scores, axis=-1, keepdims=True)
-    expon = jnp.exp(scores - row_max)
-    row_total = jnp.sum(expon, axis=-1, keepdims=True)
-    probs = (expon * (1.0 / row_total)).astype(HALF)
-    o_ref[...] = product(probs, v_ref[keys, :], ((1,), (0,))).astype(HALF)
-    lse_ref[...] = jnp.broadcast_to(row_max + jnp.log(row_total), lse_ref.shape)
-
-
-def attend(chip, q, k, v):
-    tokens, width = q.shape
-    heads = width // HD
-    return pl.pallas_call(
-        attend_kernel,
-        out_shape=[
-            jax.ShapeDtypeStruct((tokens, width), HALF),
-            jax.ShapeDtypeStruct((tokens, width), SINGLE),
-        ],
-        grid=(heads, tokens // QB),
-        in_specs=[
-            pl.BlockSpec(memory_space=pltpu.SMEM),
-            pl.BlockSpec((QB, HD), lambda h, i: (i, h)),
-            pl.BlockSpec((k.shape[0], HD), lambda h, i: (0, h)),
-            pl.BlockSpec((k.shape[0], HD), lambda h, i: (0, h)),
-        ],
-        out_specs=[
-            pl.BlockSpec((QB, HD), lambda h, i: (i, h)),
-            pl.BlockSpec((QB, HD), lambda h, i: (i, h)),
-        ],
-        compiler_params=pltpu.CompilerParams(vmem_limit_bytes=VMEM_LIMIT),
-    )(chip, q, k, v)
 
 
 def attend_back_kernel(chip_ref, q_ref, k_ref, v_ref, go_ref, lse_ref, gq_ref, gk_ref, gv_ref):
@@ -733,13 +858,13 @@
     return jnp.moveaxis(matrix.reshape(rows, 2, padded // 2), 1, 0)
 
 
+def interleave(first, second):
+    cut = lambda m: m.reshape(2, m.shape[1], -1, 1, LANES)
+    return jnp.concatenate([cut(first), cut(second)], axis=3).reshape(2, first.shape[1], -1)
+
+
 def whole(parts, width):
     return jnp.moveaxis(parts, 0, 1).reshape(parts.shape[1], -1)[:, :width]
-
-
-def rms_scale(values, gain):
-    inverse = lax.rsqrt(jnp.mean(values * values, axis=-1, keepdims=True) + EPSILON)
-    return values * inverse * gain
 
 
 def dot(a, b):
@@ -767,44 +892,25 @@
         [halves(w_query), halves(w_key), halves(w_value), gains], axis=2
     ).astype(HALF)
     chunk_out = halves(w_out.T).astype(HALF)
-    chunk_ff = jnp.concatenate([halves(w_gate), halves(w_up)], axis=2).astype(HALF)
+    chunk_ff = interleave(halves(w_gate), halves(w_up)).astype(HALF)
     chunk_down = halves(w_down.T).astype(HALF)
     ff = chunk_down.shape[-1]
-
-    *gathered, earlier, own = gather_all(
+    tokens = hidden_in.shape[0]
+
+    *gathered, a1, cots, queries, kv, attended, log_totals, mid, a2, hidden_ff, grad_ff, gain_rows = forward(
         [chunk_qkv, chunk_out, chunk_ff, chunk_down], hidden_in, out_grad
     )
     w_qkv, wo_t, w_ff, wd_t = [w.reshape(features, w.shape[-1]) for w in gathered]
-    gain_rows = w_qkv[:, 3 * heads_width :].T[:2].astype(SINGLE)
-    gain_one, gain_two = gain_rows[:1], gain_rows[1:]
+    gain_one, gain_two = gain_rows[0:1], gain_rows[1:2]
     w_qkv = w_qkv[:, : 3 * heads_width]
-    own = own.reshape(2, 512, features)
-    cot_full = own[1]
-    rows = jnp.concatenate([earlier.reshape(1024, features), own[0]])
-
-    first_in = rms_scale(rows.astype(SINGLE), gain_one).astype(HALF)
-    first_own = first_in[1024:]
-    queries = dot(first_own, w_qkv[:, :heads_width]).astype(HALF)
-    kv = dot(first_in, w_qkv[:, heads_width:]).astype(HALF)
+    cot_full = cots.reshape(512, features)
+    first_own = a1.reshape(512, features)
+    second_in = a2.reshape(512, features)
     keys, values = kv[:, :heads_width], kv[:, heads_width:]
     chip_ref = chip.reshape(1).astype(jnp.int32)
-    attended, log_totals = attend(chip_ref, queries, keys, values)
-    tokens = hidden_in.shape[0]
     rows_single = jax.ShapeDtypeStruct((tokens, features), SINGLE)
     rows_half = jax.ShapeDtypeStruct((tokens, features), HALF)
-    mid, second_in = sum_call(
-        post_mid, 1, dot_t(attended, wo_t), [hidden_in, gain_two], [rows_single], True
-    )
-    second_in = second_in.reshape(512, features)
-    gate_up = dot(second_in, w_ff)
-    gate, up_proj = gate_up[:, :ff], gate_up[:, ff:]
-    hidden_ff = (jax.nn.silu(gate) * up_proj).astype(HALF)
     (hidden_out,) = sum_call(post_out, 2, dot_t(hidden_ff, wd_t), [mid], [rows_half], False)
-    grad_hidden = dot(cot_full, wd_t)
-    sig = jax.nn.sigmoid(gate)
-    grad_gate = grad_hidden * up_proj * sig * (1.0 + gate * (1.0 - sig))
-    grad_up = grad_hidden * gate * sig
-    grad_ff = jnp.concatenate([grad_gate, grad_up], axis=1).astype(HALF)
     grad_mid, ffn_terms, grad_branch = sum_call(
         post_mid_back,
         3,
@@ -839,6 +945,8 @@
     g_qkv = t_dot(first_own, grad_qkv).astype(HALF)
     g_qkv = jnp.concatenate([g_qkv, gain_cols], axis=1)
     s_down, s_ff, s_out, s_qkv = scatter_all([g_down, g_ff, g_out, g_qkv])
+    s_ff = s_ff.reshape(2, 32, ff // LANES, 2, LANES)
+    s_gate, s_up = s_ff[:, :, :, 0].reshape(2, 32, ff), s_ff[:, :, :, 1].reshape(2, 32, ff)
     gain_sum = s_qkv[0, :, 3 * heads_width :] + s_qkv[1, :, 3 * heads_width :]
     h = heads_width
     return (
@@ -850,8 +958,8 @@
         whole(s_qkv[:, :, 2 * h : 3 * h], 2 * h),
         whole(s_out, 2 * h).T,
         gain_sum[:, 1],
-        whole(s_ff[:, :, :ff], hidden_units),
-        whole(s_ff[:, :, ff:], hidden_units),
+        whole(s_gate, hidden_units),
+        whole(s_up, hidden_units),
         whole(s_down, hidden_units).T,
     )
 

time: 752 us -> 693 us (0.922)
  matrix products: 86.4 us -> 54.4 us
  Pallas kernels: 595 us -> 577 us
  other arithmetic: 28.2 us -> 13.5 us
    dot_general x5 -> x1, matrix products: 32.5 us -> 4.42 us  [dot(): return jnp.dot(a, b, preferred_element_type=SINGLE)]
    pallas_call x2 -> x1, Pallas kernels: 232 us -> 254 us  [forward(): pl.pallas_call(forward_kernel, out_shape=[shape(full(w.shape[-1]), HALF)...]
    pallas_call x4 -> x3, Pallas kernels: 146 us -> 126 us  [sum_call(): pl.pallas_call(functools.partial(sum_kernel, post, len(ins), len(outs), s...]
    pallas_call x1, Pallas kernels: 171 us -> 151 us  [scatter_all(): pl.pallas_call(functools.partial(scatter_kernel, n), out_shape=[jax.Shape...]
    convert_element_type x2 -> x0, other arithmetic: 8.18 us -> none  [the longest x1 8.17 us: per_device(): first_in = rms_scale(rows.astype(SINGLE), gain_one).astype(HALF)]
    dot_general x8 -> x7, matrix products: 53.9 us -> 50 us  [product(): lax.dot_general(a, b, (dims, ((), ())), preferred_element_type=SINGLE)]
where the time goes in v2:
time: 693 us; the launch traced here: 683 us
  Pallas kernels  577 us (83%)
  matrix products  54.4 us (8%)
  local copies, waits for them, and re-layouts  36.3 us (5%)
  other arithmetic  13.5 us (2%)
    pallas_call x1, Pallas kernels, forward(): pl.pallas_call(forward_kernel, out_shape=[shape(full(w.shape[-1]), HALF)...  254 us
    pallas_call x1, Pallas kernels, scatter_all(): pl.pallas_call(functools.partial(scatter_kernel, n), out_shape=[jax.Shape...  151 us
    pallas_call x3, Pallas kernels, sum_call(): pl.pallas_call(functools.partial(sum_kernel, post, len(ins), len(outs), s...  126 us
    dot_general x7, matrix products, product(): lax.dot_general(a, b, (dims, ((), ())), preferred_element_type=SINGLE)  50 us
    pallas_call x1, Pallas kernels, return_call(): pl.pallas_call(return_kernel, out_shape=jax.ShapeDtypeStruct(own.shape, H...  29.9 us
    pallas_call x1, Pallas kernels, attend_back(): pl.pallas_call(attend_back_kernel, out_shape=[jax.ShapeDtypeStruct((token...  16.1 us

profile of v2, /device:TPU:1, one launch (start us, length us, event | category | flops | bytes accessed | tf_op | source)
XLA Modules:
  0.0 683.1 jit_solution(1768999822249801580)
XLA Ops:
  9.2 253.7 %shard_map.194 = (bf16[4,2,4,2,32,1664]{5,4,3,2,1,0:T(8,128)(2,1)}, bf16[4,2,4,2,32,512]{5,4,3,2,1,0:T(8,128)(2,1)}, bf16[4,2,4,2,32,2816]{5,4,3,2,1,0:T(8,128)(...) custom-call(bf16[2,32,1664]{2,1,0:T(8,128)(2,1)} %pad_maximum_fusion, ...), custom_call_target="tpu_custom_call" | custom-call | tf_op jit(solution)/shard_map/pallas_call | solution.py:438
  262.9 11.3 %fusion.10.refs_0_ = f32[2,256,2048]{2,1,0:T(8,128)} fusion(bf16[2,256,2816]{2,1,0:T(8,128)(2,1)} %bitcast.158, bf16[2048,2816,1]{1,0,2:T(8,128)(2,1)} %bitcast.153), kind=kOutput, calls=%fused_computation.43 | convolution fusion | flops 5905580032 | bytes 18612224 | tf_op jit(solution)/shard_map/dot_general | solution.py:167
  274.2 1.5 fusion.8
  275.7 37.9 %shard_map.196 = (f32[256,2048]{1,0:T(8,128)}, f32[256,2048]{1,0:T(8,128)}, bf16[2,256,2048]{2,1,0:T(8,128)(2,1)}) custom-call(f32[2,256,2048]{2,1,0:T(8,128)} %fusion.10.refs_0_, f32[256,2048]{1,0:T(8,128)} %get-tuple-element.40.refs_1_, bf16[256,2048]{1,0:T(8,128)(2,1)} %refs_2_.1, f32[1,2048]{1,0:T(1,128)} %get-tuple-element.75.refs_3_), custom_call_target="tpu_custom_call" | custom-call | tf_op jit(solution)/shard_map/pallas_call | solution.py:724
  313.6 4.4 convolution_convert_fusion.4.go_ref
  318.1 1.9 fusion.7
  320.0 16.1 %shard_map.197 = (bf16[512,512]{1,0:T(8,128)(2,1)}, f32[1536,512]{1,0:T(8,128)}, f32[1536,512]{1,0:T(8,128)}) custom-call(s32[1]{0:T(128)} %bitcast.14.chip_ref, bf16[512,512]{1,0:T(8,128)(2,1)} %get-tuple-element.41.q_ref, bf16[1536,512]{1,0:T(8,128)(2,1)} %get-tuple-element.70.k_ref, bf16[1536,512]{1,0:T(8,128)(2,1)} %get-tuple-element.69.v_ref, ...), custom_call_target="tpu_custom_call" | custom-call | tf_op jit(solution)/shard_map/pallas_call | solution.py:833
  336.0 2.5 constant_dynamic-update-slice_fusion.1
  339.2 1.6 slice.104
  342.3 29.9 %shard_map.198 = bf16[512,1024]{1,0:T(8,128)(2,1)} custom-call(f32[512,1024]{1,0:T(8,128)} %slice.81.own, bf16[2,512,1024]{2,1,0:T(8,128)(2,1)} %bitcast.123), custom_call_target="tpu_custom_call" | custom-call | tf_op jit(solution)/shard_map/pallas_call | solution.py:790
  372.3 8.0 %convolution_convert_fusion.1 = bf16[2048,1536]{0,1:T(8,128)(2,1)} fusion(bf16[512,2048]{1,0:T(8,128)(2,1)} %bitcast.161, bf16[512,1024]{1,0:T(8,128)(2,1)} %shard_map.198, bf16[512,512]{1,0:T(8,128)(2,1)S(1)} %copy-done.17), kind=kOutput, calls=%fused_computation.3 | convolution fusion | flops 3227516928 | bytes 9961472 | tf_op jit(solution)/shard_map/dot_general | solution.py:167
  380.3 5.1 fusion.2
  385.4 55.9 %shard_map.199 = (f32[256,2048]{1,0:T(8,128)}, f32[256,2048]{1,0:T(8,128)}) custom-call(f32[2,256,2048]{2,1,0:T(8,128)} %bitcast.125, bf16[256,2048]{1,0:T(8,128)(2,1)} %refs_1_.1, f32[256,2048]{1,0:T(8,128)} %get-tuple-element.53.refs_2_, f32[1,2048]{1,0:T(1,128)} %get-tuple-element.74.refs_3_), custom_call_target="tpu_custom_call" | custom-call | tf_op jit(solution)/shard_map/pallas_call | solution.py:724
  442.7 6.8 fusion.1
  449.6 9.9 %copy.72 = bf16[2048,1664]{1,0:T(8,128)(2,1)} copy(bf16[2048,1664]{0,1:T(8,128)(2,1)} %fusion.1) | data formatting | bytes 13631488 | tf_op jit(solution)/shard_map/concatenate | solution.py:946
  459.5 2.6 convolution_convert_fusion.3
  462.3 9.2 %convolution_convert_fusion = bf16[2048,2816]{1,0:T(8,128)(2,1)} fusion(bf16[512,2048]{1,0:T(8,128)(2,1)S(1)} %bitcast.160, bf16[512,2816]{1,0:T(8,128)(2,1)S(1)} %copy-done.11), kind=kOutput, calls=%fused_computation.2 | convolution fusion | flops 5911347200 | bytes 16515072 | tf_op jit(solution)/shard_map/dot_general | solution.py:167
  471.5 5.3 convolution_convert_fusion.2
  476.8 151.4 %shard_map.200 = (f32[2,32,1408]{2,1,0:T(8,128)}, f32[2,32,2816]{2,1,0:T(8,128)}, f32[2,32,512]{2,1,0:T(8,128)}, f32[2,32,1664]{2,1,0:T(8,128)}) custom-call(bf16[4,2,4,2,32,1408]{5,4,3,2,1,0:T(8,128)(2,1)} %bitcast.124, bf16[4,2,4,2,32,2816]{5,4,3,2,1,0:T(8,128)(2,1)} %bitcast.122, bf16[4,2,4,2,32,512]{5,4,3,2,1,0:T(8,128)(2,1)} %bitcast.126, ...), custom_call_target="tpu_custom_call" | custom-call | tf_op jit(solution)/shard_map/pallas_call | solution.py:643
  628.2 1.5 reshape.161
  629.6 1.9 slice_reduce_fusion
  638.0 8.5 %fusion.9.refs_0_ = f32[2,256,2048]{2,1,0:T(8,128)} fusion(bf16[2,256,1408]{2,1,0:T(8,128)(2,1)} %bitcast.165, bf16[2048,1408,1]{1,0,2:T(8,128)(2,1)} %bitcast.157), kind=kOutput, calls=%fused_computation.42 | convolution fusion | flops 2952790016 | bytes 11403264 | tf_op jit(solution)/shard_map/dot_general | solution.py:167
  646.5 32.5 %shard_map.195 = bf16[256,2048]{1,0:T(8,128)(2,1)} custom-call(f32[2,256,2048]{2,1,0:T(8,128)} %fusion.9.refs_0_, f32[256,2048]{1,0:T(8,128)} %get-tuple-element.40.refs_1_), custom_call_target="tpu_custom_call" | custom-call | tf_op jit(solution)/shard_map/pallas_call | solution.py:724
  679.0 2.3 copy.109
  (86 shorter events, 19.9 us)
Async XLA Ops:
  0.6 5.5 copy-start.6
  4.3 3.5 copy-start.7
  6.0 2.5 copy-start.9
  313.6 4.4 copy-start
  336.0 2.8 copy-start.1
  342.3 30.0 %copy-start.17 = (bf16[512,512]{1,0:T(8,128)(2,1)S(1)}, bf16[512,512]{1,0:T(8,128)(2,1)}, u32[]{:S(2)}) copy-start(bf16[512,512]{1,0:T(8,128)(2,1)} %get-tuple-element.49) | copy-start | bytes 1572868
  342.3 38.0 %slice-start = ((s8[6815744]{0:T(1024)(128)(4,1)}), s8[2621440]{0:T(1024)(128)(4,1)S(1)}, s32[]{:S(2)}) async-start(s8[6815744]{0:T(1024)(128)(4,1)} %bitcast.154), calls=%async_computation | async-start | bytes 5242880
  372.2 8.1 %copy-start.4 = (bf16[512,1024]{1,0:T(8,128)(2,1)S(1)}, bf16[512,1024]{1,0:T(8,128)(2,1)}, u32[]{:S(2)}) copy-start(bf16[512,1024]{1,0:T(8,128)(2,1)} %shard_map.198) | copy-start | bytes 3145732
  372.2 8.1 %slice-start.1 = ((s8[6815744]{0:T(1024)(128)(4,1)}), s8[4194304]{0:T(1024)(128)(4,1)S(1)}, s32[]{:S(2)}) async-start(s8[6815744]{0:T(1024)(128)(4,1)} %bitcast.154), calls=%async_computation.1 | async-start | bytes 8388608
  385.4 56.0 %copy-start.3 = (f32[256,2048]{1,0:T(8,128)S(1)}, f32[256,2048]{1,0:T(8,128)}, u32[]{:S(2)}) copy-start(f32[256,2048]{1,0:T(8,128)} %get-tuple-element.60) | copy-start | bytes 6291460
  449.5 9.9 %copy-start.14 = (bf16[2,256,2048]{2,1,0:T(8,128)(2,1)S(1)}, bf16[2,256,2048]{2,1,0:T(8,128)(2,1)}, u32[]{:S(2)}) copy-start(bf16[2,256,2048]{2,1,0:T(8,128)(2,1)} %get-tuple-element.46) | copy-start | bytes 6291460
  449.5 9.9 %copy-start.16 = (bf16[512,512]{1,0:T(8,128)(2,1)S(1)}, bf16[512,512]{1,0:T(8,128)(2,1)}, u32[]{:S(2)}) copy-start(bf16[512,512]{1,0:T(8,128)(2,1)} %get-tuple-element.57) | copy-start | bytes 1572868
  459.5 2.6 copy-start.11
  459.5 2.9 copy-start.13
  462.3 9.2 %copy-start.12 = (bf16[2,256,2048]{2,1,0:T(8,128)(2,1)S(1)}, bf16[2,256,2048]{2,1,0:T(8,128)(2,1)}, u32[]{:S(2)}) copy-start(bf16[2,256,2048]{2,1,0:T(8,128)(2,1)} %get-tuple-element.55) | copy-start | bytes 6291460
  462.3 9.2 %copy-start.15 = (bf16[512,1408]{1,0:T(8,128)(2,1)S(1)}, bf16[512,1408]{1,0:T(8,128)(2,1)}, u32[]{:S(2)}) copy-start(bf16[512,1408]{1,0:T(8,128)(2,1)} %get-tuple-element.38) | copy-start | bytes 4325380
  629.6 4.2 copy-start.8
  631.6 3.0 copy-start.5
  631.9 4.7 copy-start.10
  646.5 34.8 %copy-start.2 = (f32[256,2048]{1,0:T(8,128)S(1)}, f32[256,2048]{1,0:T(8,128)}, u32[]{:S(2)}) copy-start(f32[256,2048]{1,0:T(8,128)} %get-tuple-element.90) | copy-start | bytes 6291460

commit v3 on v0

v3 whole, which is shorter than its diff:
```python
import functools
import math

import jax
import jax.numpy as jnp
from jax import lax
from jax.experimental import pallas as pl
from jax.experimental.pallas import tpu as pltpu
from jax.sharding import PartitionSpec as P

HD = 128
WINDOW = 1024
EPSILON = 1e-06
MASKED = -1e30
MESH = pl.DeviceIdType.MESH
HALF = jnp.bfloat16
SINGLE = jnp.float32
VMEM_LIMIT = 62 * 2**20

D = 2048
TOK = 256
HW = 512
FF = 1408
QB = 256
KB = QB + WINDOW
SCALE = 1.0 / math.sqrt(HD)
ROWS = 16
LANES = 128
PART = 512
PARTS = D // PART


def coords():
    s = lax.axis_index("seq")
    t = lax.axis_index("tp")
    return lax.rem(lax.div(s, 2), 4), lax.div(s, 16), lax.rem(lax.div(s, 8), 2), lax.rem(s, 2), t


def device(x, y, z, c, t):
    return (((y * 2 + z) * 4 + x) * 2 + c, t)


def moved(v, steps):
    return lax.rem(v + steps + 4, 4)


def chip_shift(steps):
    s = lax.axis_index("seq")
    return (lax.rem(s + 2 * steps + 64, 64), lax.axis_index("tp"))


def neighbours():
    x, y, z, c, t = coords()
    return [
        device(moved(x, 1), y, z, c, t),
        device(moved(x, -1), y, z, c, t),
        device(x, moved(y, 1), z, c, t),
        device(x, moved(y, -1), z, c, t),
        device(x, y, 1 - z, c, t),
        device(x, y, z, 1 - c, t),
    ]


def window_chips():
    return [chip_shift(1), chip_shift(-1), chip_shift(2), chip_shift(-2)]


def greet(partners):
    barrier = pltpu.get_barrier_semaphore()
    for partner in partners:
        pl.semaphore_signal(barrier, inc=1, device_id=partner, device_id_type=MESH)
    pl.semaphore_wait(barrier, len(partners))


class Sems:
    def __init__(self, send, recv):
        self.send, self.recv, self.used, self.started = send, recv, 0, []

    def copy(self, src, dst, dev):
        i = self.used
        self.used += 1
        return pltpu.make_async_remote_copy(
            src, dst, self.send.at[i], self.recv.at[i], device_id=dev, device_id_type=MESH
        )

    def start(self, *copies):
        for copy in copies:
            copy.start()
            self.started.append(copy)

    def finish(self):
        for copy in self.started:
            copy.wait_send()


class Locals:
    def __init__(self, sems):
        self.sems, self.used = sems, 0

    def sem(self):
        self.used += 1
        return self.sems.at[self.used - 1]

    def copy(self, src, dst):
        return pltpu.make_async_copy(src, dst, self.sem())

    def load(self, src, dst):
        copy = self.copy(src, dst)
        copy.start()
        return copy


class Plan:
    def __init__(self):
        self.steps = []

    def add(self, when, step):
        self.steps.append((when, len(self.steps), step))

    def until(self, when):
        self.steps.sort(key=lambda s: s[:2])
        while self.steps and self.steps[0][0] <= when:
            self.steps.pop(0)[2]()

    def rest(self):
        self.until(math.inf)


def grid_piece(h):
    x, y, z, c, t = coords()
    if h == 0:
        return y, x, lambda v: device(x, v, z, c, t), lambda v: device(v, y, z, c, t)
    return x, y, lambda v: device(v, y, z, c, t), lambda v: device(x, v, z, c, t)


def blocks(ref, h, a, zs, b):
    return ref.at[a, zs, b, h] if h == 0 else ref.at[b, zs, a, h]


ALL = slice(None)


GATHER_COPIES = 1 + 2 * 13


def plan_gather(plan, begin, length, w_in, out, sems, local):
    x, y, z, c, t = coords()
    mine = local.copy(w_in.at[c], out.at[y, z, x, c])
    swap = sems.copy(w_in.at[1 - c], out.at[y, z, x, c], device(x, y, z, 1 - c, t))
    over_z, streams = [], []
    for h in range(2):
        a, b, to_a, to_b = grid_piece(h)
        src = out.at[y, z, x, h]
        over_z.append(sems.copy(src, src, device(x, y, 1 - z, c, t)))
        for s, zs, d in ((0, z, 1), (1, 1 - z, -1)):

            def copy(aa, bb, dev, h=h, zs=zs):
                src = blocks(out, h, aa, zs, bb)
                return sems.copy(src, src, dev)

            streams.append(
                dict(
                    s=s,
                    a1f=copy(a, b, to_a(moved(a, d))),
                    a1r=copy(a, b, to_a(moved(a, -d))),
                    a2=copy(moved(a, -d), b, to_a(moved(a, d))),
                    b1f=copy(ALL, b, to_b(moved(b, d))),
                    b1r=copy(ALL, b, to_b(moved(b, -d))),
                    b2=copy(ALL, moved(b, -d), to_b(moved(b, d))),
                )
            )
    first, second = [[p for p in streams if p["s"] == s] for s in range(2)]

    def first_start():
        mine.start()
        sems.start(swap)

    def own():
        mine.wait()
        swap.wait_recv()
        sems.start(*over_z)
        for p in first:
            sems.start(p["a1f"], p["a1r"])

    def other():
        for copy in over_z:
            copy.wait_recv()
        for p in second:
            sems.start(p["a1f"], p["a1r"])

    def a2(ps):
        for p in ps:
            p["a1f"].wait_recv()
            sems.start(p["a2"])

    def b1(ps):
        for p in ps:
            p["a1r"].wait_recv()
            p["a2"].wait_recv()
            sems.start(p["b1f"], p["b1r"])

    def b2(ps):
        for p in ps:
            p["b1f"].wait_recv()
            sems.start(p["b2"])

    def end(ps):
        for p in ps:
            p["b1r"].wait_recv()
            p["b2"].wait_recv()

    first_start()
    plan.add(begin - 24, own)
    plan.add(begin - 20, other)
    plan.add(begin - 16, lambda: a2(first))
    plan.add(begin - 12, lambda: a2(second))
    plan.add(begin - 6, lambda: b1(first))
    plan.add(begin - 2, lambda: b1(second))
    plan.add(begin + 0.4 * length, lambda: b2(first))
    plan.add(begin + 0.55 * length, lambda: b2(second))
    plan.add(begin + length, lambda: end(first))
    plan.add(begin + length, lambda: end(second))


SCATTER_COPIES = 4 * 6 + 3
SCATTER_LOADS = 16


def scatter_slots(w):
    return [
        jax.ShapeDtypeStruct((2, 2, 4, 32, w), HALF),
        jax.ShapeDtypeStruct((2, 2, 2, 4, 32, w), HALF),
    ]


def scatter_scratch(w):
    return [
        pltpu.VMEM((2, 2, 4, 32, w), HALF),
        pltpu.VMEM((2, 2, 4, 32, w), HALF),
        pltpu.VMEM((2, 2, 32, w), HALF),
        pltpu.VMEM((2, 2, 2, 32, w), HALF),
        pltpu.VMEM((2, 32, w), HALF),
        pltpu.VMEM((2, 32, w), SINGLE),
    ]


def plus(ref, *others):
    total = ref[...].astype(SINGLE)
    for other in others:
        total = total + other[...].astype(SINGLE)
    ref[...] = total.astype(HALF)


def plan_scatter(plan, begin, length, g, out, slots, scratch, temp, sems, local):
    x, y, z, c, t = coords()
    r2, r1 = slots
    tt, ss, q2, q1, rz, final = scratch
    width = g.shape[-1]
    wide = slice(0, width)
    streams = []
    for h in range(2):
        a, b, to_a, to_b = grid_piece(h)
        for s, zs, d in ((0, z, 1), (1, 1 - z, -1)):
            at_g = lambda bb, h=h, zs=zs: blocks(g, h, ALL, zs, bb)
            tmp = temp.at[h, s, :, :, :, wide]
            streams.append(
                dict(
                    h=h,
                    s=s,
                    a=a,
                    d=d,
                    load_t=local.copy(at_g(moved(b, d)), tt.at[h, s]),
                    load_s=local.copy(at_g(b), ss.at[h, s]),
                    load_2=local.copy(r2.at[h, s], tmp.at[0]),
                    load_1=local.copy(r1.at[h, s], tmp),
                    x2=sems.copy(at_g(moved(b, 2)), r2.at[h, s], to_b(moved(b, d))),
                    x1r=sems.copy(at_g(moved(b, -d)), r1.at[h, s, 1], to_b(moved(b, -d))),
                    x1f=sems.copy(tt.at[h, s], r1.at[h, s, 0], to_b(moved(b, d))),
                    y2=sems.copy(ss.at[h, s, moved(a, 2)], q2.at[h, s], to_a(moved(a, d))),
                    y1r=sems.copy(ss.at[h, s, moved(a, -d)], q1.at[h, s, 1], to_a(moved(a, -d))),
                    y1f=sems.copy(ss.at[h, s, moved(a, d)], q1.at[h, s, 0], to_a(moved(a, d))),
                )
            )
    over_z = [
        sems.copy(ss.at[h, 1, grid_piece(h)[0]], rz.at[h], device(x, y, 1 - z, c, t))
        for h in range(2)
    ]
    swap = sems.copy(final.at[1 - c], out.at[c], device(x, y, z, 1 - c, t))

    def start():
        for p in streams:
            sems.start(p["x2"], p["x1r"])
        for p in streams:
            p["load_t"].start()
            p["load_s"].start()

    def x1():
        for p in streams:
            p["load_t"].wait()
            p["x2"].wait_recv()
            p["load_2"].start()
        for p in streams:
            h, s = p["h"], p["s"]
            p["load_2"].wait()

            def body(i, carry, h=h, s=s):
                plus(tt.at[h, s, i], temp.at[h, s, 0, i, :, wide])
                return carry

            lax.fori_loop(0, 4, body, 0)
            sems.start(p["x1f"])

    def x0():
        for p in streams:
            p["load_s"].wait()
            p["x1r"].wait_recv()
            p["x1f"].wait_recv()
            p["load_1"].start()
        for p in streams:
            h, s = p["h"], p["s"]
            p["load_1"].wait()

            def body(i, carry, h=h, s=s):
                plus(
                    ss.at[h, s, i], temp.at[h, s, 0, i, :, wide], temp.at[h, s, 1, i, :, wide]
                )
                return carry

            lax.fori_loop(0, 4, body, 0)
            sems.start(p["y2"], p["y1r"])

    def y1():
        for p in streams:
            h, s = p["h"], p["s"]
            p["y2"].wait_recv()
            plus(ss.at[h, s, moved(p["a"], p["d"])], q2.at[h, s])
            sems.start(p["y1f"])

    def y0():
        for p in streams:
            h, s = p["h"], p["s"]
            p["y1f"].wait_recv()
            p["y1r"].wait_recv()
            plus(ss.at[h, s, p["a"]], q1.at[h, s, 0], q1.at[h, s, 1])
            if s == 1:
                sems.start(over_z[h])

    def last():
        for p in streams:
            h = p["h"]
            if p["s"] == 0:
                over_z[h].wait_recv()
                final[h] = ss[h, 0, p["a"]].astype(SINGLE) + rz[h].astype(SINGLE)
        out[c] = final[c]
        sems.start(swap)

    plan.add(begin, start)
    plan.add(begin + 0.4 * length, x1)
    plan.add(begin + length, x0)
    plan.add(begin + length + 4, y1)
    plan.add(begin + length + 8, y0)
    plan.add(begin + length + 12, last)
    plan.add(begin + length + 16, swap.wait_recv)


def make_grads(lhs, rhs_columns, staging, g, local):
    sems = [local.sem() for _ in range(2)]

    def write(i, slot):
        return pltpu.make_async_copy(staging.at[slot], g.at[i, slot], sems[slot])

    def body(i, carry):
        for slot in range(2):
            n = pl.multiple_of(i * 512 + slot * 256, 256)
            left = lhs[:, :, pl.ds(n, 256)].reshape(512, 256)
            tile = product(left, rhs_columns(), ((0,), (0,))).astype(HALF)

            @pl.when(i > 0)
            def _():
                write(i, slot).wait()

            staging[slot] = tile.reshape(staging.shape[1:])
            write(i, slot).start()
        return carry

    lax.fori_loop(0, 4, body, 0)
    for slot in range(2):
        write(0, slot).wait()


class FourSum:
    def __init__(self, bufs, sems):
        x, y, z, c, t = coords()
        self.to_core, self.from_core, self.to_pair, self.from_pair, self.own = bufs
        self.sems = sems
        self.cols = [slice(i * PART, (i + 1) * PART) for i in range(PARTS)]
        core, pair = device(x, y, z, 1 - c, t), device(x, y, z, c, 1 - t)
        self.core = [sems.copy(self.to_core.at[:, n], self.from_core.at[:, n], core) for n in self.cols]
        self.pair = [sems.copy(self.to_pair.at[:, n], self.from_pair.at[:, n], pair) for n in self.cols]

    def put(self, i, theirs, ours):
        self.to_core[:, self.cols[i]] = theirs.astype(HALF)
        self.own[:, self.cols[i]] = ours
        self.sems.start(self.core[i])

    def relay(self, i):
        n = self.cols[i]
        self.core[i].wait_recv()

        def add(r):
            self.to_pair[r, n] = (self.own[r, n] + self.from_core[r, n].astype(SINGLE)).astype(HALF)

        row_loop(0, TOK, add, 64)
        self.sems.start(self.pair[i])

    def wait(self):
        for copy in self.pair:
            copy.wait_recv()

    def total(self, r):
        return self.to_pair[r, :].astype(SINGLE) + self.from_pair[r, :].astype(SINGLE)


SUM_COPIES = 2 * PARTS
SUM_SCRATCH = [pltpu.VMEM((TOK, D), HALF) for _ in range(4)] + [pltpu.VMEM((TOK, D), SINGLE)]


def product(a, b, dims):
    return lax.dot_general(a, b, (dims, ((), ())), preferred_element_type=SINGLE)


def allowed_pairs(base):
    row = lax.broadcasted_iota(jnp.int32, (QB, KB), 0)
    col = lax.broadcasted_iota(jnp.int32, (QB, KB), 1)
    return (col > row) & (col <= row + WINDOW) & (col + base >= 0)


def attend_block(q, k, v, base):
    scores = product(q, k, ((1,), (1,))) * SCALE
    scores = jnp.where(allowed_pairs(base), scores, MASKED)
    row_max = jnp.max(scores, axis=-1, keepdims=True)
    expon = jnp.exp(scores - row_max)
    row_total = jnp.sum(expon, axis=-1, keepdims=True)
    probs = (expon * (1.0 / row_total)).astype(HALF)
    mixed = product(probs, v, ((1,), (0,))).astype(HALF)
    return mixed, row_max + jnp.log(row_total)


def attend_block_back(q, k, v, go, lse, base):
    scores = product(q, k, ((1,), (1,))) * SCALE
    scores = jnp.where(allowed_pairs(base), scores, MASKED)
    probs = jnp.exp(scores - lse)
    gp = product(go, v, ((1,), (1,)))
    inner = jnp.sum(probs * gp, axis=-1, keepdims=True)
    gs = (probs * (gp - inner)).astype(HALF)
    gq = product(gs, k, ((1,), (0,))) * SCALE
    gk = product(gs, q, ((0,), (0,))) * SCALE
    gv = product(probs.astype(HALF), go, ((0,), (0,)))
    return gq, gk, gv


def rms_inverse(values):
    return lax.rsqrt(jnp.mean(values * values, axis=-1, keepdims=True) + EPSILON)


def norm_back(grad, values, gain):
    inverse = rms_inverse(values)
    scaled = grad * gain
    slope = jnp.mean(scaled * values, axis=-1, keepdims=True)
    gain_term = jnp.sum(grad * values * inverse, axis=0, keepdims=True)
    return inverse * scaled - values * (inverse * inverse * inverse * slope), gain_term


def row_loop(start, count, fn, step=ROWS):
    def body(i, carry):
        fn(pl.ds(pl.multiple_of(start + i * step, step), step))
        return carry

    lax.fori_loop(0, count // step, body, 0)


def columns(w, n, size):
    return w[:, :, :, :, :, pl.ds(n, size)].reshape(D, size)


def pick_lanes():
    return lax.broadcasted_iota(jnp.int32, (8, LANES), 0) == lax.broadcasted_iota(
        jnp.int32, (8, LANES), 1
    )


ANYWHERE = pl.BlockSpec(memory_space=pl.ANY)
IN_VMEM = pl.BlockSpec(memory_space=pltpu.VMEM)
SHAPE = jax.ShapeDtypeStruct


def grid_of(w):
    return (4, 2, 4, 2, 32, w)


def params(collective_id):
    return pltpu.CompilerParams(
        collective_id=collective_id, has_side_effects=True, vmem_limit_bytes=VMEM_LIMIT
    )


W_QKV, W_OUT, W_FF, W_DOWN = range(4)
GATHER_TIMES = ((24, 34), (58, 10), (68, 58), (126, 29))


def forward_kernel(*refs):
    w_in, (hid, cot) = refs[:4], refs[4:6]
    w_out = refs[6:10]
    a1, cots, q, kv, o, lse, mid, a2, hid_ff, grad_ff, gains = refs[10:21]
    rows, w_qkv, w_o, w_ff, cot_v, gate_up = refs[21:27]
    send, recv, local_sems = refs[32:]
    x, y, z, c, t = coords()
    chip = lax.div(lax.axis_index("seq"), 2)
    core, pair = device(x, y, z, 1 - c, t), device(x, y, z, c, 1 - t)
    sems, local = Sems(send, recv), Locals(local_sems)
    greet(neighbours() + [pair] + window_chips())

    plan = Plan()
    for i in range(4):
        plan_gather(plan, *GATHER_TIMES[i], w_in[i], w_out[i], sems, local)
    row_copy = local.load(hid, rows.at[c])
    cot_copy = local.load(cot, cots.at[c])
    row_swap = sems.copy(hid, rows.at[c], core)
    cot_swap = sems.copy(cot, cots.at[c], core)
    sems.start(row_swap, cot_swap)

    plan.until(sum(GATHER_TIMES[W_QKV]))
    load_qkv = local.load(w_out[W_QKV], w_qkv)
    row_copy.wait()
    row_swap.wait_recv()
    load_qkv.wait()
    pick = pick_lanes().astype(HALF)
    gains[...] = product(pick, columns(w_qkv, 3 * HW, LANES), ((1,), (1,)))

    for half in range(2):

        def norm_one(r, half=half):
            values = rows[half, r, :].astype(SINGLE)
            a1[half, r, :] = (values * rms_inverse(values) * gains[0:1, :]).astype(HALF)

        row_loop(0, TOK, norm_one)
    plan.until(62)

    def project(n):
        w_cols = columns(w_qkv, n, 2 * HD)
        return [product(a1[half], w_cols, ((1,), (0,))).astype(HALF) for half in range(2)]

    halo = []
    for h in range(4):
        n = slice(h * 2 * HD, (h + 1) * 2 * HD)
        out = project(HW + h * 2 * HD)
        for half in range(2):
            kv[WINDOW + half * TOK : WINDOW + (half + 1) * TOK, n] = out[half]
        own = kv.at[1024:1536, n]
        copies = [
            sems.copy(own, kv.at[512:1024, n], chip_shift(1)),
            sems.copy(own, kv.at[0:512, n], chip_shift(2)),
        ]
        sems.start(*copies)
        halo.append(copies)
    for n in range(0, HW, 2 * HD):
        out = project(n)
        for half in range(2):
            q[half * TOK : (half + 1) * TOK, n : n + 2 * HD] = out[half]
    plan.until(74)
    load_o = local.load(w_out[W_OUT], w_o)
    for h in range(4):
        for copy in halo[h]:
            copy.wait_recv()
        head = slice(h * HD, (h + 1) * HD)
        key_head = slice(2 * h * HD, (2 * h + 1) * HD)
        value_head = slice((2 * h + 1) * HD, (2 * h + 2) * HD)

        def attend_one(i, carry):
            mine = pl.ds(pl.multiple_of(i * QB, QB), QB)
            keys = pl.ds(pl.multiple_of(i * QB, QB), KB)
            base = (chip - 2) * 512 + i * QB
            mixed, total = attend_block(
                q[mine, head], kv[keys, key_head], kv[keys, value_head], base
            )
            o[mine, head] = mixed
            lse[mine, head] = jnp.broadcast_to(total, (QB, HD))
            return carry

        lax.fori_loop(0, 2, attend_one, 0)
        plan.until(80 + 4 * h)
    load_o.wait()

    attended = FourSum(refs[27:32], sems)
    theirs, ours = [pl.ds(pl.multiple_of(k * TOK, TOK), TOK) for k in (1 - c, c)]
    for i in range(PARTS):
        w_rows = w_o[i].reshape(PART, HW)
        attended.put(
            i,
            product(o[theirs, :], w_rows, ((1,), (1,))),
            product(o[ours, :], w_rows, ((1,), (1,))),
        )
    for i in range(PARTS):
        attended.relay(i)
    plan.until(104)
    attended.wait()
    spreads = []
    for half in range(2):

        def norm_two(r):
            values = rows[c, r, :].astype(SINGLE) + attended.total(r)
            mid[r, :] = values
            a2[c, r, :] = (values * rms_inverse(values) * gains[1:2, :]).astype(HALF)

        row_loop(half * 128, 128, norm_two)
        part = a2.at[c, half * 128 : (half + 1) * 128]
        copy = sems.copy(part, part, core)
        sems.start(copy)
        spreads.append(copy)
    plan.until(sum(GATHER_TIMES[W_FF]))
    load_ff = local.load(w_out[W_FF], w_ff)
    for copy in spreads:
        copy.wait_recv()
    load_ff.wait()

    def gate_and_up(i, carry):
        n = pl.multiple_of(i * 2 * LANES, 2 * LANES)
        w_cols = columns(w_ff, n, 2 * LANES)
        for half in range(2):
            r = slice(half * TOK, (half + 1) * TOK)
            both = product(a2[half], w_cols, ((1,), (0,)))
            gate_up[r, pl.ds(n, 2 * LANES)] = both
            gate, up_part = both[:, :LANES], both[:, LANES:]
            hid_part = gate / (1.0 + jnp.exp(-gate)) * up_part
            hid_ff[r, pl.ds(pl.multiple_of(i * LANES, LANES), LANES)] = hid_part.astype(HALF)
        return carry

    lax.fori_loop(0, FF // LANES, gate_and_up, 0)
    plan.rest()
    load_down = local.load(w_out[W_DOWN], w_qkv.at[:, :, :, :, :, 0:FF])
    cot_copy.wait()
    cot_swap.wait_recv()
    load_cot = local.load(cots, cot_v)
    load_cot.wait()
    load_down.wait()

    def back(i, carry):
        w_cols = columns(w_qkv, pl.multiple_of(i * LANES, LANES), LANES)
        n = pl.multiple_of(i * 2 * LANES, 2 * LANES)
        for half in range(2):
            r = slice(half * TOK, (half + 1) * TOK)
            ghid = product(cot_v[half], w_cols, ((1,), (0,)))
            gate = gate_up[r, pl.ds(n, LANES)]
            up_part = gate_up[r, pl.ds(n + LANES, LANES)]
            sig = 1.0 / (1.0 + jnp.exp(-gate))
            grad_ff[r, pl.ds(n, LANES)] = (
                ghid * up_part * sig * (1.0 + gate * (1.0 - sig))
            ).astype(HALF)
            grad_ff[r, pl.ds(n + LANES, LANES)] = (ghid * gate * sig).astype(HALF)
        return carry

    lax.fori_loop(0, FF // LANES, back, 0)
    sems.finish()


def forward(chunks, hid, cot):
    copies = GATHER_COPIES * 4 + 2 + 8 + SUM_COPIES + 2
    return pl.pallas_call(
        forward_kernel,
        out_shape=[SHAPE(grid_of(w.shape[-1]), HALF) for w in chunks]
        + [
            SHAPE((2, TOK, D), HALF),
            SHAPE((2, TOK, D), HALF),
            SHAPE((2 * TOK, HW), HALF),
            SHAPE((WINDOW + 2 * TOK, 2 * HW), HALF),
            SHAPE((2 * TOK, HW), HALF),
            SHAPE((2 * TOK, HW), SINGLE),
            SHAPE((TOK, D), SINGLE),
            SHAPE((2, TOK, D), HALF),
            SHAPE((2 * TOK, FF), HALF),
            SHAPE((2 * TOK, 2 * FF), HALF),
            SHAPE((8, D), SINGLE),
        ],
        in_specs=[ANYWHERE] * 6,
        out_specs=[ANYWHERE] * 4 + [IN_VMEM, ANYWHERE] + [IN_VMEM] * 9,
        scratch_shapes=[
            pltpu.VMEM((2, TOK, D), HALF),
            pltpu.VMEM(grid_of(chunks[W_QKV].shape[-1]), HALF),
            pltpu.VMEM(grid_of(HW), HALF),
            pltpu.VMEM(grid_of(2 * FF), HALF),
            pltpu.VMEM((2, TOK, D), HALF),
            pltpu.VMEM((2 * TOK, 2 * FF), SINGLE),
        ]
        + SUM_SCRATCH
        + [
            pltpu.SemaphoreType.DMA((copies,)),
            pltpu.SemaphoreType.DMA((copies,)),
            pltpu.SemaphoreType.DMA((4 + 2 + 5,)),
        ],
        compiler_params=params(0),
    )(*chunks, hid, cot)


def backward_kernel(*refs):
    (
        w_ff,
        w_out,
        cots,
        hid_in,
        grad_ff_in,
        a2_in,
        mid_in,
        gains,
        q_in,
        kv_in,
        lse_in,
    ) = refs[:11]
    s_down, s_ffa, s_ffb, gmid, gatt, gq, gkv, ffn_term = refs[11:19]
    g_refs, slot_refs = refs[19:22], refs[22:28]
    rest = refs[28:]
    scatter_bufs, rest = [rest[6 * i : 6 * i + 6] for i in range(3)], rest[18:]
    sum_bufs, rest = rest[:5], rest[5:]
    (
        temp,
        staging,
        cot_v,
        hid_ff,
        grad_ff,
        a2,
        mid,
        q,
        kv,
        lse,
        w_tiles,
        w_o,
        go,
        acc,
        own_kv,
        far,
        got,
        send,
        recv,
        local_sems,
    ) = rest
    x, y, z, c, t = coords()
    chip = lax.div(lax.axis_index("seq"), 2)
    core, pair = device(x, y, z, 1 - c, t), device(x, y, z, c, 1 - t)
    sems, local = Sems(send, recv), Locals(local_sems)
    loads = {
        name: local.load(src, dst)
        for name, src, dst in (
            ("grad_ff", grad_ff_in, grad_ff),
            ("cot", cots, cot_v),
            ("hid", hid_in, hid_ff),
            ("a2", a2_in, a2),
            ("mid", mid_in, mid),
            ("w_o", w_out, w_o),
            ("q", q_in, q),
            ("kv", kv_in, kv),
            ("lse", lse_in, lse),
        )
    }
    tiles = [local.copy(w_ff.at[i // 2, i % 2], w_tiles.at[i % 2]) for i in range(8)]
    tiles[0].start()
    tiles[1].start()
    greet(neighbours() + [pair] + window_chips())

    plan = Plan()
    for i, (begin, length, out) in enumerate(((1, 30, s_down), (2, 58, s_ffa), (3, 86, s_ffb))):
        plan_scatter(
            plan,
            begin,
            length,
            g_refs[i],
            out,
            slot_refs[2 * i : 2 * i + 2],
            scatter_bufs[i],
            temp,
            sems,
            local,
        )

    loads["grad_ff"].wait()
    gn2 = FourSum(sum_bufs, sems)
    theirs, ours = [pl.ds(pl.multiple_of(k * TOK, TOK), TOK) for k in (1 - c, c)]
    for i in range(PARTS):
        parts = []
        for k in range(2):
            tiles[2 * i + k].wait()
            w_rows = w_tiles[k].reshape(256, 2 * FF)
            parts.append(
                [product(grad_ff[r, :], w_rows, ((1,), (1,))) for r in (theirs, ours)]
            )
            if 2 * i + k + 2 < 8:
                tiles[2 * i + k + 2].start()
        gn2.put(i, *[jnp.concatenate([parts[0][j], parts[1][j]], axis=1) for j in range(2)])

    loads["cot"].wait()
    loads["hid"].wait()
    make_grads(cot_v, lambda: hid_ff[...], staging, g_refs[0], local)
    plan.until(1)
    for i in range(PARTS):
        gn2.relay(i)
    loads["a2"].wait()
    make_grads(a2, lambda: grad_ff[:, :FF], staging, g_refs[1], local)
    plan.until(2)
    make_grads(a2, lambda: grad_ff[:, FF:], staging, g_refs[2], local)
    plan.until(14)

    gn2.wait()
    loads["mid"].wait()
    ffn_term[...] = jnp.zeros_like(ffn_term)
    spreads = []
    for half in range(2):

        def mid_back(r):
            part, term = norm_back(gn2.total(r), mid[r, :], gains[1:2, :])
            grad = cot_v[c, r, :].astype(SINGLE) + part
            gmid[r, :] = grad
            gatt[c, r, :] = grad.astype(HALF)
            ffn_term[0:1, :] += term

        row_loop(half * 128, 128, mid_back)
        part = gatt.at[c, half * 128 : (half + 1) * 128]
        copy = sems.copy(part, part, core)
        sems.start(copy)
        spreads.append(copy)
    plan.until(20)
    loads["w_o"].wait()
    for copy in spreads:
        copy.wait_recv()
    for half in range(2):
        total = product(gatt[half, :, 0:PART], w_o[0].reshape(PART, HW), ((1,), (0,)))
        for i in range(1, PARTS):
            total += product(
                gatt[half, :, i * PART : (i + 1) * PART], w_o[i].reshape(PART, HW), ((1,), (0,))
            )
        go[half * TOK : (half + 1) * TOK, :] = total.astype(HALF)
    for name in ("q", "kv", "lse"):
        loads[name].wait()
    returns = []
    for h in range(4):
        head = slice(h * HD, (h + 1) * HD)
        both = slice(2 * h * HD, (2 * h + 2) * HD)
        key_head = slice(2 * h * HD, (2 * h + 1) * HD)
        value_head = slice((2 * h + 1) * HD, (2 * h + 2) * HD)
        acc[...] = jnp.zeros_like(acc)

        def attend_one(i, carry):
            mine = pl.ds(pl.multiple_of(i * QB, QB), QB)
            keys = pl.ds(pl.multiple_of(i * QB, QB), KB)
            base = (chip - 2) * 512 + i * QB
            grad_q, grad_k, grad_v = attend_block_back(
                q[mine, head],
                kv[keys, key_head],
                kv[keys, value_head],
                go[mine, head],
                lse[mine, h * HD : h * HD + 1],
                base,
            )
            gq[mine, head] = grad_q.astype(HALF)
            acc[keys, 0:HD] += grad_k
            acc[keys, HD:] += grad_v
            return carry

        lax.fori_loop(0, 2, attend_one, 0)
        copies = []
        for j, shift in ((1, -1), (0, -2)):
            far[j, :, both] = acc[512 * j : 512 * (j + 1), :].astype(HALF)
            copies.append(sems.copy(far.at[j, :, both], got.at[j, :, both], chip_shift(shift)))
        sems.start(*copies)
        returns.append(copies)
        own_kv[:, both] = acc[1024:1536, :]
        plan.until(26 + 5 * h)
    for h in range(4):
        both = slice(2 * h * HD, (2 * h + 2) * HD)
        for copy in returns[h]:
            copy.wait_recv()

        def add(r):
            total = (
                own_kv[r, both] + got[1, r, both].astype(SINGLE) + got[0, r, both].astype(SINGLE)
            )
            gkv[r, both] = total.astype(HALF)

        row_loop(0, 512, add, 64)
        plan.until(46 + 5 * h)
    plan.rest()
    sems.finish()


def backward(w_ff, w_out, cots, hid_ff, grad_ff, a2, mid, gains, q, kv, lse):
    widths = (FF, FF, FF)
    copies = SCATTER_COPIES * 3 + SUM_COPIES + 2 + 8
    slots = [slot for w in widths for slot in scatter_slots(w)]
    return pl.pallas_call(
        backward_kernel,
        out_shape=[SHAPE((2, 32, w), SINGLE) for w in widths]
        + [
            SHAPE((TOK, D), SINGLE),
            SHAPE((2, TOK, D), HALF),
            SHAPE((2 * TOK, HW), HALF),
            SHAPE((2 * TOK, 2 * HW), HALF),
            SHAPE((8, D), SINGLE),
        ]
        + [SHAPE(grid_of(w), HALF) for w in widths]
        + slots,
        in_specs=[ANYWHERE] * 7 + [IN_VMEM] + [ANYWHERE] * 3,
        out_specs=[IN_VMEM] * 8 + [ANYWHERE] * (3 + len(slots)),
        scratch_shapes=[buf for w in widths for buf in scatter_scratch(w)]
        + SUM_SCRATCH
        + [
            pltpu.VMEM((2, 2, 2, 4, 32, FF), HALF),
            pltpu.VMEM((2, 4, 2, 32, FF), HALF),
            pltpu.VMEM((2, TOK, D), HALF),
            pltpu.VMEM((2 * TOK, FF), HALF),
            pltpu.VMEM((2 * TOK, 2 * FF), HALF),
            pltpu.VMEM((2, TOK, D), HALF),
            pltpu.VMEM((TOK, D), SINGLE),
            pltpu.VMEM((2 * TOK, HW), HALF),
            pltpu.VMEM((WINDOW + 2 * TOK, 2 * HW), HALF),
            pltpu.VMEM((2 * TOK, HW), SINGLE),
            pltpu.VMEM((2, 4, 2, 32, 2 * FF), HALF),
            pltpu.VMEM(grid_of(HW), HALF),
            pltpu.VMEM((2 * TOK, HW), HALF),
            pltpu.VMEM((WINDOW + 2 * TOK, 2 * HD), SINGLE),
            pltpu.VMEM((2 * TOK, 2 * HW), SINGLE),
            pltpu.VMEM((2, 2 * TOK, 2 * HW), HALF),
            pltpu.VMEM((2, 2 * TOK, 2 * HW), HALF),
            pltpu.SemaphoreType.DMA((copies,)),
            pltpu.SemaphoreType.DMA((copies,)),
            pltpu.SemaphoreType.DMA((9 + 8 + SCATTER_LOADS * 3 + 2 * 3,)),
        ],
        compiler_params=params(1),
    )(w_ff, w_out, cots, hid_ff, grad_ff, a2, mid, gains, q, kv, lse)


def finish_kernel(*refs):
    w_qkv, w_down, a1_in, gq, gkv, gatt, o, hid_ff, mid, gmid, hid, gains, ffn_term = refs[:13]
    s_out, s_qkv, s_gain, in_grad, hidden_out = refs[13:18]
    g_refs, slot_refs = refs[18:21], refs[21:27]
    rest = refs[27:]
    scatter_bufs, rest = [rest[6 * i : 6 * i + 6] for i in range(3)], rest[18:]
    in_bufs, out_bufs, rest = rest[:5], rest[5:10], rest[10:]
    temp, staging, staging_o, gqkv, gain_acc, a1, w_tiles, d_tiles, send, recv, local_sems = rest
    x, y, z, c, t = coords()
    core, pair = device(x, y, z, 1 - c, t), device(x, y, z, c, 1 - t)
    sems, local = Sems(send, recv), Locals(local_sems)
    load_a1 = local.load(a1_in, a1)
    w_loads = [
        local.copy(w_qkv.at[i // 2, i % 2, :, :, :, 0 : 3 * HW], w_tiles.at[i % 2])
        for i in range(8)
    ]
    d_loads = [local.copy(w_down.at[i // 2, i % 2], d_tiles.at[i % 2]) for i in range(8)]
    for load in (*w_loads[:2], *d_loads[:2]):
        load.start()
    gqkv[:, :HW] = gq[...]
    gqkv[:, HW:] = gkv[...]
    greet(neighbours() + [pair])
    plan = Plan()
    for i, (begin, length, out) in enumerate(((1, 12, s_out), (0, 42, s_qkv), (30, 25, s_gain))):
        plan_scatter(
            plan,
            begin,
            length,
            g_refs[i],
            out,
            slot_refs[2 * i : 2 * i + 2],
            scatter_bufs[i],
            temp,
            sems,
            local,
        )
    load_a1.wait()
    make_grads(a1, lambda: gqkv[...], staging, g_refs[1], local)
    plan.until(0)
    theirs, ours = [pl.ds(pl.multiple_of(k * TOK, TOK), TOK) for k in (1 - c, c)]

    def partial_sum(bufs, left, right, loads, depth):
        total = FourSum(bufs, sems)
        for i in range(PARTS):
            parts = []
            for k in range(2):
                loads[2 * i + k].wait()
                w_rows = right[k].reshape(256, depth)
                parts.append([product(left[r, :], w_rows, ((1,), (1,))) for r in (theirs, ours)])
                if 2 * i + k + 2 < 8:
                    loads[2 * i + k + 2].start()
            total.put(i, *[jnp.concatenate([parts[0][j], parts[1][j]], axis=1) for j in range(2)])
        return total

    gn1 = partial_sum(in_bufs, gqkv, w_tiles, w_loads, 3 * HW)
    make_grads(gatt, lambda: o[...], staging_o, g_refs[0], local)
    plan.until(2)
    for i in range(PARTS):
        gn1.relay(i)
    out_sum = partial_sum(out_bufs, hid_ff, d_tiles, d_loads, FF)
    plan.until(6)
    for i in range(PARTS):
        out_sum.relay(i)
    plan.until(18)
    gn1.wait()
    gain_acc[...] = jnp.zeros_like(gain_acc)

    def rows_back(r):
        part, term = norm_back(gn1.total(r), hid[r, :].astype(SINGLE), gains[0:1, :])
        in_grad[r, :] = gmid[r, :] + part
        gain_acc[0:1, :] += term

    row_loop(0, TOK, rows_back)
    gain_acc[1:2, :] = ffn_term[0:1, :]
    pick = pick_lanes().astype(HALF)
    for n in range(8):
        cols = product(
            gain_acc[:, n * 256 : (n + 1) * 256].astype(HALF), pick, ((0,), (0,))
        ).astype(HALF)
        staging_o[0, :, :, :, 0:LANES] = cols.reshape(4, 2, 32, LANES)
        copy = local.load(staging_o.at[0, :, :, :, 0:LANES], g_refs[2].at[n // 2, n % 2])
        copy.wait()
    plan.until(30)
    out_sum.wait()

    def rows_out(r):
        hidden_out[r, :] = (mid[r, :] + out_sum.total(r)).astype(HALF)

    row_loop(0, TOK, rows_out)
    plan.rest()
    sems.finish()


def finish(w_qkv, w_down, a1, gq, gkv, gatt, o, hid_ff, mid, gmid, hid, gains, ffn_term):
    widths = (HW, 3 * HW, LANES)
    copies = SCATTER_COPIES * 3 + SUM_COPIES * 2
    slots = [slot for w in widths for slot in scatter_slots(w)]
    return pl.pallas_call(
        finish_kernel,
        out_shape=[SHAPE((2, 32, w), SINGLE) for w in widths]
        + [SHAPE((TOK, D), SINGLE), SHAPE((TOK, D), HALF)]
        + [SHAPE(grid_of(w), HALF) for w in widths]
        + slots,
        in_specs=[ANYWHERE] * 3 + [IN_VMEM] * 10,
        out_specs=[IN_VMEM] * 5 + [ANYWHERE] * (3 + len(slots)),
        scratch_shapes=[buf for w in widths for buf in scatter_scratch(w)]
        + SUM_SCRATCH
        + SUM_SCRATCH
        + [
            pltpu.VMEM((2, 2, 2, 4, 32, 3 * HW), HALF),
            pltpu.VMEM((2, 4, 2, 32, 3 * HW), HALF),
            pltpu.VMEM((2, 4, 2, 32, HW), HALF),
            pltpu.VMEM((2 * TOK, 3 * HW), HALF),
            pltpu.VMEM((8, D), SINGLE),
            pltpu.VMEM((2, TOK, D), HALF),
            pltpu.VMEM((2, 4, 2, 32, 3 * HW), HALF),
            pltpu.VMEM((2, 4, 2, 32, FF), HALF),
            pltpu.SemaphoreType.DMA((copies,)),
            pltpu.SemaphoreType.DMA((copies,)),
            pltpu.SemaphoreType.DMA((1 + 8 + 8 + SCATTER_LOADS * 3 + 2 * 2 + 8,)),
        ],
        compiler_params=params(2),
    )(w_qkv, w_down, a1, gq, gkv, gatt, o, hid_ff, mid, gmid, hid, gains, ffn_term)


def halves(matrix):
    rows, width = matrix.shape
    padded = -(-width // 256) * 256
    matrix = jnp.pad(matrix, ((0, 0), (0, padded - width)))
    return jnp.moveaxis(matrix.reshape(rows, 2, padded // 2), 1, 0)


def interleave(first, second):
    cut = lambda m: m.reshape(2, m.shape[1], -1, 1, LANES)
    return jnp.concatenate([cut(first), cut(second)], axis=3).reshape(2, first.shape[1], -1)


def apart(both):
    cut = both.reshape(2, both.shape[1], -1, 2, LANES)
    return [cut[:, :, :, i].reshape(2, both.shape[1], -1) for i in range(2)]


def whole(parts, width):
    return jnp.moveaxis(parts, 0, 1).reshape(parts.shape[1], -1)[:, :width]


def per_device(
    hidden_in, attn_gain, w_query, w_key, w_value, w_out, ffn_gain, w_gate, w_up, w_down, out_grad
):
    hidden_units = w_gate.shape[1]
    gains = jnp.pad(jnp.stack([attn_gain, ffn_gain], axis=1), ((0, 0), (0, LANES - 2)))
    gains = jnp.broadcast_to(gains, (2, *gains.shape))
    chunk_qkv = jnp.concatenate(
        [halves(w_query), interleave(halves(w_key), halves(w_value)), gains], axis=2
    ).astype(HALF)
    chunk_out = halves(w_out.T).astype(HALF)
    chunk_ff = interleave(halves(w_gate), halves(w_up)).astype(HALF)
    chunk_down = halves(w_down.T).astype(HALF)

    w_qkv, w_o, w_ff, w_d, a1, cots, q, kv, o, lse, mid, a2, hid_ff, grad_ff, gain_rows = forward(
        [chunk_qkv, chunk_out, chunk_ff, chunk_down], hidden_in, out_grad
    )
    s_down, s_ffa, s_ffb, gmid, gatt, gq, gkv, ffn_term, *_ = backward(
        w_ff, w_o, cots, hid_ff, grad_ff, a2, mid, gain_rows, q, kv, lse
    )
    s_out, s_qkv, s_gain, in_grad, hidden_out, *_ = finish(
        w_qkv, w_d, a1, gq, gkv, gatt, o, hid_ff, mid, gmid, hidden_in, gain_rows, ffn_term
    )
    gain_sum = s_gain[0] + s_gain[1]
    s_key, s_value = apart(s_qkv[:, :, HW:])
    s_gate, s_up = apart(jnp.concatenate([s_ffa, s_ffb], axis=2))
    return (
        hidden_out,
        in_grad,
        gain_sum[:, 0],
        whole(s_qkv[:, :, :HW], 2 * HW),
        whole(s_key, 2 * HW),
        whole(s_value, 2 * HW),
        whole(s_out, 2 * HW).T,
        gain_sum[:, 1],
        whole(s_gate, hidden_units),
        whole(s_up, hidden_units),
        whole(s_down, hidden_units).T,
    )


def solution(mesh):
    placed = (
        P("seq", None),
        P("seq"),
        P("seq", "tp"),
        P("seq", "tp"),
        P("seq", "tp"),
        P("tp", "seq"),
        P("seq"),
        P("seq", "tp"),
        P("seq", "tp"),
        P("tp", "seq"),
        P("seq", None),
    )
    return jax.shard_map(
        per_device,
        mesh=mesh,
        in_specs=placed,
        out_specs=(
            P("seq", None),
            P("seq", None),
            P("seq"),
            P("seq", "tp"),
            P("seq", "tp"),
            P("seq", "tp"),
            P("tp", "seq"),
            P("seq"),
            P("seq", "tp"),
            P("seq", "tp"),
            P("tp", "seq"),
        ),
        check_vma=False,
    )
```

time: 3470 us -> 554 us (0.16)
  waiting for transfers between devices: 2760 us -> 0 us
  Pallas kernels: 0 us -> 524 us
  blocking collectives: 416 us -> 0 us
  matrix products: 173 us -> 0 us
  other arithmetic: 42.4 us -> 5.33 us
    reduce_scatter x7 -> x0, waiting for transfers between devices: 1870 us -> none  [the longest x1 323 us: per_device(): lax.psum_scatter(down_term, 'seq', scatter_dimension=1, tiled=True)]
    all_gather x7 -> x0, waiting for transfers between devices: 632 us -> none  [the longest x1 165 us: per_device(): lax.all_gather(w_query.astype(half), 'seq', axis=0, tiled=True)]
    pallas_call x0 -> x3, Pallas kernels: none -> 524 us  [the longest x1 225 us: forward(): pl.pallas_call(forward_kernel, out_shape=[SHAPE(grid_of(w.shape[-1]), HAL...]
    unnamed x2 -> x0, blocking collectives: 416 us -> none
    psum x3 -> x0, waiting for transfers between devices: 225 us -> none  [pair_total(): return lax.psum(partial_value, 'tp')]
    dot_general x27 -> x0, matrix products: 173 us -> none  [the longest x1 13.3 us: per_device(): jnp.einsum('td,fd->tf', grad_ffn, down_back, preferred_element_type=single)]
  transfers between devices with their start and end apart: 25 -> 0, of which waited for: 20 -> 0; matrix products, arithmetic and copies ran while one was open for 5% -> 0% of each run, Pallas kernels for 0% -> 0%
where the time goes in v3:
time: 554 us; the launch traced here: 550 us
  Pallas kernels  524 us (95%)
  local copies, waits for them, and re-layouts  19.7 us (4%)
    pallas_call x1, Pallas kernels, forward(): pl.pallas_call(forward_kernel, out_shape=[SHAPE(grid_of(w.shape[-1]), HAL...  225 us
    pallas_call x1, Pallas kernels, backward(): pl.pallas_call(backward_kernel, out_shape=[SHAPE((2, 32, w), SINGLE) for...  183 us
    pallas_call x1, Pallas kernels, finish(): pl.pallas_call(finish_kernel, out_shape=[SHAPE((2, 32, w), SINGLE) for w...  115 us

profile of v3, /device:TPU:1, one launch (start us, length us, event | category | flops | bytes accessed | tf_op | source)
XLA Modules:
  0.0 550.0 jit_solution(9439357992016805581)
XLA Ops:
  0.7 0.7 pad_maximum_fusion.4
  1.5 0.9 convert.44
  2.5 1.0 convert.45
  3.5 0.9 convert.46
  4.7 0.7 pad_maximum_fusion.2.refs_0_
  7.0 0.9 convert_element_type.28.refs_2_
  8.0 0.7 copy.104
  8.7 225.0 %shard_map.194 = (bf16[4,2,4,2,32,1664]{5,4,3,2,1,0:T(8,128)(2,1)}, bf16[4,2,4,2,32,512]{5,4,3,2,1,0:T(8,128)(2,1)}, bf16[4,2,4,2,32,2816]{5,4,3,2,1,0:T(8,128)(...) custom-call(bf16[2,32,1664]{2,1,0:T(8,128)(2,1)} %pad_maximum_fusion, ...), custom_call_target="tpu_custom_call" | custom-call | tf_op jit(solution)/shard_map/pallas_call | solution.py:668
  233.7 183.5 %shard_map.195 = (f32[2,32,1408]{2,1,0:T(8,128)}, f32[2,32,1408]{2,1,0:T(8,128)}, f32[2,32,1408]{2,1,0:T(8,128)}, f32[256,2048]{1,0:T(8,128)}, bf16[2,256,2048]{...) custom-call(bf16[4,2,4,2,32,2816]{5,4,3,2,1,0:T(8,128)(2,1)} %get-tu, ...), custom_call_target="tpu_custom_call" | custom-call | tf_op jit(solution)/shard_map/pallas_call | solution.py:896
  417.2 115.3 %shard_map.196 = (f32[2,32,512]{2,1,0:T(8,128)}, f32[2,32,1536]{2,1,0:T(8,128)}, f32[2,32,128]{2,1,0:T(8,128)}, f32[256,2048]{1,0:T(8,128)}, bf16[256,2048]{1,0:...) custom-call(bf16[4,2,4,2,32,1664]{5,4,3,2,1,0:T(8,128)(2,1)} %get-tu, ...), custom_call_target="tpu_custom_call" | custom-call | tf_op jit(solution)/shard_map/pallas_call | solution.py:1035
  532.5 0.8 add_bitcast_fusion
  533.3 0.7 slice_reduce_fusion.4
  534.0 1.6 copy.91
  535.5 0.9 slice_bitcast_fusion.1
  536.4 1.0 slice.43
  538.3 0.7 slice_reduce_fusion.2
  539.2 0.7 copy.94
  540.1 0.7 copy.93
  540.8 0.8 slice_bitcast_fusion
  542.0 1.9 slice_reduce_fusion
  544.2 0.8 copy.96
  545.4 0.8 copy.95
  546.1 2.3 copy.113
  548.4 1.3 copy.114
  (54 shorter events, 4.4 us)
Async XLA Ops:
  0.6 5.4 copy-start.1
  0.7 4.8 copy-start.7
  2.5 3.8 copy-start.2
  6.3 1.6 copy-start.3
  532.5 8.3 %copy-start.4 = (f32[2,32,1408]{2,1,0:T(8,128)S(1)}, f32[2,32,1408]{2,1,0:T(8,128)}, u32[]{:S(2)}) copy-start(f32[2,32,1408]{2,1,0:T(8,128)} %get-tuple-element.66) | copy-start | bytes 1081348
  537.4 4.1 copy-start.5
  537.4 4.1 copy-start.6
  545.0 3.4 copy-start
